TPU v7x, 32 devices: a whole 2x2x4 slice. The times are simulated.
32 devices in a mesh: row: 8 (over z, x), col: 4 (over y, core).
Axes of the slice: x: 2, y: 2, z: 4, core: 2. Of those that a mesh axis runs over, the one named last changes fastest.
Arguments:
- features: bfloat16 [4096, 256], P(('row', 'col')), may hold values from -6 to 6
- weight: bfloat16 [256, 256], replicated, may hold values from -0.375 to 0.375
- cotangent: bfloat16 [4096, 256], P(('row', 'col')), may hold values from -6 to 6
- adjacency_tiles: bfloat16 [8, 4, 8, 128, 128], P('row', 'col'), as said below
- tile_coords: int32 [8, 4, 8, 2], P('row', 'col'), may hold values from 0 to 7, as said below
- tile_counts: int32 [8, 4], P('row', 'col'), may hold values from 1 to 8, as said below
Outputs:
- activations: bfloat16 [4096, 256], P(('row', 'col'))
- weight_grad: float32 [256, 256], replicated
- input_grad: bfloat16 [4096, 256], P(('row', 'col'))
Inputs may be any that keep to these rules, and one draw needn't show every extreme that they name: `adjacency_tiles`: edge weights are nonnegative. `tile_coords`: entry 0 of a slot is a tile row below 4, entry 1 a tile column below 8; the live slots of one block name distinct tiles. `tile_counts`: some block has exactly 8 live slots.
All inputs are finite; a program needn't handle non-finite values.
Results may differ from a plain program's by a relative error of at most 0.03.
Values may be sent and summed in bfloat16 or wider, within the bound.
No kernel may reach another device: no remote copies, remote signals or barrier semaphores. Data moves between devices by JAX's collectives and lax.ppermute only.
A program may use at most 128 MiB of HBM per device.

v0:
```python
import math

import jax
import jax.numpy as jnp
from jax import lax
from jax.sharding import PartitionSpec as P


def slot_products(totals, tile_block, coord_block, active, source, flipped):
    if flipped:
        picked = jnp.take(source, coord_block[:, 0], axis=0)
        products = jnp.einsum(
            "bij,bif->bjf", tile_block, picked, preferred_element_type=jnp.float32
        )
        target = coord_block[:, 1]
    else:
        picked = jnp.take(source, coord_block[:, 1], axis=0)
        products = jnp.einsum(
            "bij,bjf->bif", tile_block, picked, preferred_element_type=jnp.float32
        )
        target = coord_block[:, 0]
    products = jnp.where(active[:, None, None], products, 0.0)
    return totals.at[target].add(products)


def apply_tiles(totals, adjacency, coordinates, live_count, source, flipped, block_size):
    rounds = (live_count + block_size - 1) // block_size

    def advance(block_index, running):
        offset = block_index * block_size
        tile_block = lax.dynamic_slice_in_dim(adjacency, offset, block_size, 0)
        coord_block = lax.dynamic_slice_in_dim(coordinates, offset, block_size, 0)
        active = offset + jnp.arange(block_size, dtype=jnp.int32) < live_count
        return slot_products(running, tile_block, coord_block, active, source, flipped)

    return lax.fori_loop(0, rounds, advance, totals)


def body(features, weight, cotangent, adjacency_tiles, tile_coords, tile_counts):
    node_dev = features.shape[0]
    width = features.shape[1]
    tile_size = adjacency_tiles.shape[-1]
    capacity = adjacency_tiles.shape[2]
    row_count = lax.axis_size("row")
    col_count = lax.axis_size("col")
    tile_rows = node_dev * col_count // tile_size
    tile_cols = node_dev * row_count // tile_size
    block_size = math.gcd(32, capacity)
    adjacency = adjacency_tiles[0, 0]
    coordinates = tile_coords[0, 0]
    live_count = tile_counts[0, 0]
    gathered = lax.all_gather(features, "row", axis=0, tiled=True)
    column_source = gathered.reshape(tile_cols, tile_size, width)
    row_zeros = jnp.zeros((tile_rows, tile_size, width), jnp.float32)
    row_partial = apply_tiles(
        row_zeros, adjacency, coordinates, live_count, column_source, False, block_size
    )
    summed = lax.psum_scatter(
        row_partial.reshape(tile_rows * tile_size, width).astype(jnp.bfloat16),
        "col",
        scatter_dimension=0,
        tiled=True,
    )
    preact = jnp.dot(summed, weight, preferred_element_type=jnp.float32)
    sigmoid_z = jax.nn.sigmoid(preact)
    activations = (preact * sigmoid_z).astype(jnp.bfloat16)
    grad_pre = (
        cotangent.astype(jnp.float32) * sigmoid_z * (1.0 + preact * (1.0 - sigmoid_z))
    ).astype(jnp.bfloat16)
    local_grad = lax.dot_general(
        summed, grad_pre, (((0,), (0,)), ((), ())), preferred_element_type=jnp.float32
    )
    weight_grad = lax.psum(local_grad, ("row", "col"))
    grad_agg = lax.dot_general(
        grad_pre, weight, (((1,), (1,)), ((), ())), preferred_element_type=jnp.float32
    ).astype(jnp.bfloat16)
    row_gathered = lax.all_gather(grad_agg, "col", axis=0, tiled=True)
    row_source = row_gathered.reshape(tile_rows, tile_size, width)
    col_zeros = jnp.zeros((tile_cols, tile_size, width), jnp.float32)
    col_partial = apply_tiles(
        col_zeros, adjacency, coordinates, live_count, row_source, True, block_size
    )
    column_total = lax.psum_scatter(
        col_partial.reshape(tile_cols * tile_size, width).astype(jnp.bfloat16),
        "row",
        scatter_dimension=0,
        tiled=True,
    )
    return (activations, weight_grad, column_total)


def solution(mesh):
    return jax.shard_map(
        body,
        mesh=mesh,
        in_specs=(
            P(("row", "col"), None),
            P(),
            P(("row", "col"), None),
            P("row", "col", None, None, None),
            P("row", "col", None, None),
            P("row", "col"),
        ),
        out_specs=(P(("row", "col"), None), P(), P(("row", "col"), None)),
        check_vma=False,
    )
```

profile of v0, /device:TPU:0, one launch (start us, length us, event | category | flops | bytes accessed | tf_op | source)
XLA Modules:
  0.0 275.9 jit_solution(17767414562000716734)
XLA Ops:
  7.2 0.0 copy-start
  7.2 0.0 reduce-scatter.3.cloned.1.call-start
  7.9 0.0 copy-start.2
  7.9 0.7 copy-done.2
  8.6 33.2 %all_gather.6 = bf16[1024,256]{1,0:T(8,128)(2,1)S(1)} all-gather(bf16[128,256]{1,0:T(8,128)(2,1)} %param.10), channel_id=1, replica_groups=mesh['row'=8,'col'=4] {'row'}, dimensions={0}, use_global_device_ids=true | all-gather | bytes 589824 | tf_op jit(solution)/shard_map/all_gather | solution.py:52
  41.8 0.6 gather_fusion.1
  42.4 0.3 copy.15
  42.8 3.7 %while.22 = (s32[]{:T(128)}, f32[4,128,256]{2,1,0:T(8,128)S(1)}, s32[]{:T(128)}, s32[8,2]{0,1:T(2,128)S(1)}, s32[]{:T(128)}, /*index=5*/bf16[8,128,256]{1,2,0:T(...) while((s32[]{:T(128)}, f32[4,128,256]{2,1,0:T(8,128)S(1)}, s32[]{:T(128)}, ...), condition=%wide.region_2.3_spmd, body=%wide.region_0.2_spmd.sunk | while | flops 67895384 | bytes 7078161 | solution.py:36
  42.8 0.7 add_compare_fusion.4
  43.5 1.3 fusion.34
  44.8 0.3 copy.19
  45.1 1.3 scatter_fusion
  46.4 0.7 convert_element_type.24
  47.2 0.0 copy-start.3
  47.2 0.0 reduce-scatter.3.cloned.1.call-update
  47.2 0.0 all-reduce.2.cloned.1.call-start
  47.3 21.2 %reduce-scatter.3.cloned.1.call-done = bf16[128,256]{1,0:T(8,128)(2,1)} async-done(((bf16[512,256]{1,0:T(8,128)(2,1)}), bf16[128,256]{1,0:T(8,128)(2,1)}) %reduce-scatter.3.cloned.1.call-update) | async-done | bytes 65552 | tf_op jit(solution)/shard_map/reduce_scatter | solution.py:58
  68.5 0.0 copy-done
  68.5 0.0 copy-done.3
  68.5 1.7 multiply_convert_fusion
  70.2 0.2 convolution_convert_fusion
  70.4 0.0 copy-start.1
  70.4 5.9 %all_gather.7 = bf16[512,256]{1,0:T(8,128)(2,1)S(1)} all-gather(bf16[128,256]{1,0:T(8,128)(2,1)S(1)} %convolution_convert_fusion), channel_id=1, replica_groups=mesh['row'=8,'col'=4] {'col'}, dimensions={0}, use_global_device_ids=true | all-gather | bytes 327680 | tf_op jit(solution)/shard_map/all_gather | solution.py:77
  76.3 0.0 copy-done.1
  76.3 0.9 fusion.14
  77.2 0.0 all-reduce.2.cloned.1.call-update
  77.3 0.0 reduce-scatter.5.cloned.1.call-start
  77.3 0.1 broadcast_in_dim.60
  77.4 4.4 %while.23 = (s32[]{:T(128)}, f32[8,128,256]{2,1,0:T(8,128)S(1)}, s32[]{:T(128)}, s32[8,2]{0,1:T(2,128)S(1)}, s32[]{:T(128)}, /*index=5*/bf16[4,128,256]{2,1,0:T(...) while((s32[]{:T(128)}, f32[8,128,256]{2,1,0:T(8,128)S(1)}, s32[]{:T(128)}, ...), condition=%wide.region_7.8_spmd, body=%wide.region_5.7_spmd.sunk | while | flops 67896432 | bytes 8130961 | solution.py:36
  77.4 0.6 gather_fusion
  78.0 0.7 add_compare_fusion.5
  78.7 1.4 fusion.38
  80.1 0.3 copy.20
  80.4 1.3 scatter_fusion.1
  81.8 0.8 convert_element_type.30
  82.6 0.0 reduce-scatter.5.cloned.1.call-update
  82.6 119.8 %all-reduce.2.cloned.1.call-done = f32[256,256]{1,0:T(8,128)} async-done(((f32[256,256]{1,0:T(8,128)}), f32[256,256]{1,0:T(8,128)}) %all-reduce.2.cloned.1.call-update) | async-done | bytes 262160 | tf_op jit(solution)/shard_map/psum | solution.py:73
  202.5 65.2 %reduce-scatter.5.cloned.1.call-done = bf16[128,256]{1,0:T(8,128)(2,1)} async-done(((bf16[1024,256]{1,0:T(8,128)(2,1)}), bf16[128,256]{1,0:T(8,128)(2,1)}) %reduce-scatter.5.cloned.1.call-update) | async-done | bytes 65552 | tf_op jit(solution)/shard_map/reduce_scatter | solution.py:83
  267.7 1.7 copy.39
  (8 shorter events, 0.1 us)
Async XLA Ops:
  7.2 61.3 %copy-start = (bf16[256,256]{1,0:T(8,128)(2,1)S(1)}, bf16[256,256]{1,0:T(8,128)(2,1)}, u32[]{:S(2)}) copy-start(bf16[256,256]{1,0:T(8,128)(2,1)} %param.11) | copy-start | bytes 393220
  7.2 61.3 %reduce-scatter.3.cloned.1.call-start = ((), (), s32[]{:S(2)}) async-start(), calls=%async_computation.2 | async-start | bytes 327680 | tf_op jit(solution)/shard_map/reduce_scatter | solution.py:58
  7.9 0.7 copy-start.2
  47.2 21.3 %copy-start.3 = (bf16[128,256]{1,0:T(8,128)(2,1)S(1)}, bf16[128,256]{1,0:T(8,128)(2,1)}, u32[]{:S(2)}) copy-start(bf16[128,256]{1,0:T(8,128)(2,1)} %param.12) | copy-start | bytes 196612
  47.2 155.2 %all-reduce.2.cloned.1.call-start = ((), (), s32[]{:S(2)}) async-start(), calls=%async_computation.3 | async-start | bytes 524288 | tf_op jit(solution)/shard_map/psum | solution.py:73
  70.4 5.9 %copy-start.1 = (bf16[128,256]{1,0:T(8,128)(2,1)S(1)}, bf16[128,256]{1,0:T(8,128)(2,1)}, u32[]{:S(2)}) copy-start(bf16[128,256]{1,0:T(8,128)(2,1)} %reduce-scatter.3.cloned.1.call-done) | copy-start | bytes 196612
  77.3 190.4 %reduce-scatter.5.cloned.1.call-start = ((), (), s32[]{:S(2)}) async-start(), calls=%async_computation.4 | async-start | bytes 589824 | tf_op jit(solution)/shard_map/reduce_scatter | solution.py:83
Sparse Core Ops, SparseCore 0:
  47.3 21.1 reduce-scatter.2
  77.4 125.0 all-reduce.1
  206.7 60.8 reduce-scatter.4
where the time goes:
time: 276 us
  waiting for transfers between devices  206 us (75%)
  blocking collectives  39.1 us (14%)
  between operations  14.5 us (5%)
  other arithmetic  5.57 us (2%)
  matrix products  5.45 us (2%)
  local copies, waits for them, and re-layouts  4.58 us (2%)
    psum x1, waiting for transfers between devices, body(): weight_grad = lax.psum(local_grad, ('row', 'col'))  120 us
    reduce_scatter x1, waiting for transfers between devices, body(): lax.psum_scatter(col_partial.reshape(tile_cols * tile_size, width).astype...  65.2 us
    all_gather x1, blocking collectives, body(): gathered = lax.all_gather(features, 'row', axis=0, tiled=True)  33.2 us
    reduce_scatter x1, waiting for transfers between devices, body(): lax.psum_scatter(row_partial.reshape(tile_rows * tile_size, width).astype...  21.2 us
    all_gather x1, blocking collectives, body(): row_gathered = lax.all_gather(grad_agg, 'col', axis=0, tiled=True)  5.92 us
  transfers between devices with their start and end apart: 3, of which 3 were waited for; matrix products, arithmetic and copies ran while one was open for 2% of the time, Pallas kernels for 0%

commit v1 on v0

v1 whole, which is shorter than its diff:
```python
import functools

import jax
import jax.numpy as jnp
from jax import lax
from jax.experimental import pallas as pl
from jax.experimental.pallas import tpu as pltpu
from jax.sharding import PartitionSpec as P

F32 = jnp.float32
BF16 = jnp.bfloat16
VMEM = pl.BlockSpec(memory_space=pltpu.VMEM)
SMEM = pl.BlockSpec(memory_space=pltpu.SMEM)
VMEM_LIMIT = 16 * 1024 * 1024


def swap(value, axis, bits):
    size = lax.axis_size(axis)
    return lax.ppermute(value, axis, [(i, i ^ bits) for i in range(size)])


def call(kernel, outs, in_specs, scratch=(), flops=0):
    return pl.pallas_call(
        kernel,
        out_shape=outs,
        in_specs=in_specs,
        out_specs=jax.tree.map(lambda _: VMEM, outs),
        scratch_shapes=list(scratch),
        compiler_params=pltpu.CompilerParams(vmem_limit_bytes=VMEM_LIMIT),
        cost_estimate=pl.CostEstimate(flops=flops, bytes_accessed=0, transcendentals=0),
    )


def shape(rows, width, dtype=BF16):
    return jax.ShapeDtypeStruct((rows, width), dtype)


def block(ref, k, tile):
    return ref[k * tile:(k + 1) * tile, :]


def tile_loop(coords, count, tiles, source, total, flipped):
    row, col = lax.axis_index("row"), lax.axis_index("col")
    total[...] = jnp.zeros_like(total)

    def step(s, carry):
        r = coords[0, 0, s, 0] ^ col
        c = coords[0, 0, s, 1] ^ row
        if flipped:
            total[c] += lax.dot_general(
                tiles[0, 0, s], source[r], (((0,), (0,)), ((), ())), preferred_element_type=F32
            )
        else:
            total[r] += jnp.dot(tiles[0, 0, s], source[c], preferred_element_type=F32)
        return carry

    lax.fori_loop(0, count[0, 0], step, 0)


def forward_kernel(coords, count, tiles, *refs, tile):
    parts, (keep, send, source, total) = refs[:-4], refs[-4:]
    for slot, part in enumerate(parts):
        source[slot] = part[...]
    tile_loop(coords, count, tiles, source, total, False)
    for k in range(total.shape[0] // 2):
        keep[k * tile:(k + 1) * tile, :] = total[2 * k].astype(BF16)
        send[k * tile:(k + 1) * tile, :] = total[2 * k + 1].astype(BF16)


def backward_kernel(coords, count, tiles, mine, other, keep, send, source, total, *, tile):
    for k in range(source.shape[0] // 2):
        source[2 * k] = block(mine, k, tile)
        source[2 * k + 1] = block(other, k, tile)
    tile_loop(coords, count, tiles, source, total, True)
    for k in range(total.shape[0] // 2):
        keep[k * tile:(k + 1) * tile, :] = total[2 * k].astype(BF16)
        send[k * tile:(k + 1) * tile, :] = total[2 * k + 1].astype(BF16)


def add_kernel(a, b, out, *, flip, tile):
    for k in range(out.shape[0] // tile):
        total = block(a, k, tile).astype(F32) + block(b, k ^ flip, tile).astype(F32)
        out[k * tile:(k + 1) * tile, :] = total.astype(BF16)


def split_kernel(a, b, *outs, tile):
    for k, out in enumerate(outs):
        out[...] = (block(a, k, tile).astype(F32) + block(b, k, tile).astype(F32)).astype(BF16)


def sum_kernel(*refs):
    total = refs[0][...].astype(F32)
    for ref in refs[1:-1]:
        total += ref[...].astype(F32)
    refs[-1][...] = total.astype(refs[-1].dtype)


def dense_kernel(half, other, weight, *refs, flip, tile, share):
    cots, (act, out, kept, agg, gpre) = refs[:-5], refs[-5:]
    blocks = len(cots)
    add_kernel(half, other, agg, flip=flip, tile=tile)
    col = lax.axis_index("col")
    for k in range(blocks):
        rows = slice(k * tile, (k + 1) * tile)
        pre = jnp.dot(agg[rows, :], weight[...], preferred_element_type=F32)
        sig = jax.nn.sigmoid(pre)
        if k == 0:
            act[...] = (pre * sig).astype(BF16)
        gpre[rows, :] = (cots[k][...].astype(F32) * sig * (1.0 + pre * (1.0 - sig))).astype(BF16)
    grad = lax.dot_general(
        gpre[...], weight[...], (((1,), (1,)), ((), ())), preferred_element_type=F32
    )
    out[:blocks * tile, :] = grad.astype(BF16)
    full = lax.dot_general(
        agg[...], gpre[...], (((0,), (0,)), ((), ())), preferred_element_type=F32
    ).astype(BF16)
    wide = full.shape[0] // share
    for j in range(wide):
        @pl.when(col == j)
        def _():
            kept[...] = full[j * share:(j + 1) * share, :]
            peer = j ^ 1
            out[blocks * tile:, :] = full[peer * share:(peer + 1) * share, :]


def place_kernel(*refs, share):
    parts, out = refs[:-1], refs[-1]
    col = lax.axis_index("col")
    for slot, part in enumerate(parts):
        start = pl.multiple_of((col ^ slot) * share, share)
        out[pl.ds(start, share), :] = part[...].astype(F32)


def body(features, weight, cotangent, adjacency_tiles, tile_coords, tile_counts):
    tile, width = features.shape
    n_row, n_col = lax.axis_size("row"), lax.axis_size("col")
    half = n_col // 2
    share = weight.shape[0] // n_col
    sparse = (SMEM, SMEM, VMEM)
    adjacency = (tile_coords, tile_counts, adjacency_tiles)

    far = {m: swap(features, "row", m) for m in range(2, n_row, 2)}
    near = swap(features, "row", 1)
    parts = [features, near]
    for m in range(2, n_row, 2):
        parts += [far[m], swap(far[m], "row", 1)]
    cots = [cotangent] + [swap(cotangent, "col", 2 * k) for k in range(1, half)]

    keep, send = call(
        functools.partial(forward_kernel, tile=tile),
        [shape(half * tile, width)] * 2,
        [*sparse, *[VMEM] * n_row],
        [pltpu.VMEM((n_row, tile, width), BF16), pltpu.VMEM((n_col, tile, width), F32)],
    )(*adjacency, *parts)
    other = swap(send, "col", 1)
    partial = call(
        functools.partial(add_kernel, flip=0, tile=tile), shape(half * tile, width), [VMEM] * 2
    )(keep, other)
    bit = 1
    while bit < half:
        other = swap(partial, "col", 2 * bit)
        if 2 * bit < half:
            partial = call(
                functools.partial(add_kernel, flip=bit, tile=tile), shape(half * tile, width), [VMEM] * 2
            )(partial, other)
        bit *= 2

    act, out, kept = call(
        functools.partial(dense_kernel, flip=half // 2, tile=tile, share=share),
        [shape(tile, width), shape(half * tile + share, width), shape(share, width)],
        [VMEM] * (3 + half),
        [pltpu.VMEM((half * tile, width), BF16)] * 2,
    )(partial, other, weight, *cots)
    back = swap(out, "col", 1)

    keep, send = call(
        functools.partial(backward_kernel, tile=tile),
        [shape(n_row // 2 * tile, width)] * 2,
        [*sparse, VMEM, VMEM],
        [pltpu.VMEM((n_col, tile, width), BF16), pltpu.VMEM((n_row, tile, width), F32)],
    )(*adjacency, out, back)
    other = swap(send, "row", 1)

    def total(values, dtype=BF16):
        return call(sum_kernel, shape(*values[0].shape, dtype), [VMEM] * len(values))(*values)

    grad = total([kept, back[half * tile:]])
    grad = total([grad] + [swap(grad, "row", m) for m in range(2, n_row, 2)])
    grad = total([grad, swap(grad, "row", 1)])
    shares = [grad] + [swap(grad, "col", k) for k in range(1, n_col)]
    weight_grad = call(
        functools.partial(place_kernel, share=share),
        shape(*weight.shape, F32),
        [VMEM] * n_col,
    )(*shares)

    pieces = call(
        functools.partial(split_kernel, tile=tile), [shape(tile, width)] * (n_row // 2), [VMEM] * 2
    )(keep, other)
    input_grad = total([pieces[0]] + [swap(p, "row", 2 * k) for k, p in enumerate(pieces) if k])
    return act, weight_grad, input_grad


def solution(mesh):
    return jax.shard_map(
        body,
        mesh=mesh,
        in_specs=(
            P(("row", "col"), None),
            P(),
            P(("row", "col"), None),
            P("row", "col", None, None, None),
            P("row", "col", None, None),
            P("row", "col"),
        ),
        out_specs=(P(("row", "col"), None), P(), P(("row", "col"), None)),
        check_vma=False,
    )
```

time: 276 us -> 58.5 us (0.21)
  waiting for transfers between devices: 206 us -> 22.7 us
  blocking collectives: 39.1 us -> 0 us
  starting transfers between devices: 0.12 us -> 26.1 us
  between operations: 14.5 us -> 1.41 us
  other arithmetic: 5.57 us -> 0 us
  matrix products: 5.45 us -> 0 us
  Pallas kernels: 0 us -> 4.74 us
    psum x1 -> x0, waiting for transfers between devices: 120 us -> none  [body(): weight_grad = lax.psum(local_grad, ('row', 'col'))]
    reduce_scatter x2 -> x0, waiting for transfers between devices: 86.5 us -> none  [the longest x1 65.2 us: body(): lax.psum_scatter(col_partial.reshape(tile_cols * tile_size, width).astype...]
    all_gather x2 -> x0, blocking collectives: 39.1 us -> none  [the longest x1 33.2 us: body(): gathered = lax.all_gather(features, 'row', axis=0, tiled=True)]
    ppermute x0 -> x22, starting transfers between devices: none -> 26.1 us  [swap(): return lax.ppermute(value, axis, [(i, i ^ bits) for i in range(size)])]
    ppermute x0 -> x22, waiting for transfers between devices: none -> 22.7 us  [swap(): return lax.ppermute(value, axis, [(i, i ^ bits) for i in range(size)])]
    dot_general x5 -> x0, matrix products: 5.45 us -> none  [the longest x1 1.69 us: body(): preact = jnp.dot(summed, weight, preferred_element_type=jnp.float32)]
    pallas_call x0 -> x10, Pallas kernels: none -> 4.74 us  [the longest x1 1.13 us: body(): call(functools.partial(backward_kernel, tile=tile), [shape(n_row // 2 * t...]
  transfers between devices with their start and end apart: 3 -> 22, of which waited for: 3 -> 10; matrix products, arithmetic and copies ran while one was open for 2% -> 1% of each run, Pallas kernels for 0% -> 1%
where the time goes in v1:
time: 58.5 us; the launch traced here: 57.4 us
  starting transfers between devices  26.1 us (45%)
  waiting for transfers between devices  22.7 us (39%)
  Pallas kernels  4.74 us (8%)
  local copies, waits for them, and re-layouts  2.56 us (4%)
  between operations  1.41 us (2%)
    ppermute x22, starting transfers between devices, swap(): return lax.ppermute(value, axis, [(i, i ^ bits) for i in range(size)])  26.1 us
    ppermute x22, waiting for transfers between devices, swap(): return lax.ppermute(value, axis, [(i, i ^ bits) for i in range(size)])  22.7 us
    unnamed x11, local copies, waits for them, and re-layouts  2.56 us
  transfers between devices with their start and end apart: 22, of which 10 were waited for; matrix products, arithmetic and copies ran while one was open for 1% of the time, Pallas kernels for 1%

profile of v1, /device:TPU:0, one launch (start us, length us, event | category | flops | bytes accessed | tf_op | source)
XLA Modules:
  0.0 57.4 jit_solution(4759683005687709473)
XLA Ops:
  0.6 3.1 %collective-permute-start.1 = (bf16[128,256]{1,0:T(8,128)(2,1)}, bf16[128,256]{1,0:T(8,128)(2,1)S(1)}, u32[]{:S(2)}, u32[]{:S(2)}) collective-permute-start(bf16[128,256]{1,0:T(8,128)(2,1)} %refs_0_.2), channel_id=1, source_target_pairs={{0,8},{4,12},{8,0},{12,4},{16,24},{20,28},{24,16},{28,20},{1,9},{5... | collective-permute-start | bytes 196616 | tf_op jit(solution)/shard_map/ppermute | solution.py:19
  3.7 2.6 %collective-permute-start.3 = (bf16[128,256]{1,0:T(8,128)(2,1)}, bf16[128,256]{1,0:T(8,128)(2,1)S(1)}, u32[]{:S(2)}, u32[]{:S(2)}) collective-permute-start(bf16[128,256]{1,0:T(8,128)(2,1)} %refs_0_.2), channel_id=1, source_target_pairs={{0,16},{4,20},{8,24},{12,28},{16,0},{20,4},{24,8},{28,12},{1,17},{... | collective-permute-start | bytes 196616 | tf_op jit(solution)/shard_map/ppermute | solution.py:19
  6.3 0.0 collective-permute-start.5
  6.3 1.7 %collective-permute-start = (bf16[128,256]{1,0:T(8,128)(2,1)}, bf16[128,256]{1,0:T(8,128)(2,1)S(1)}, u32[]{:S(2)}, u32[]{:S(2)}) collective-permute-start(bf16[128,256]{1,0:T(8,128)(2,1)} %refs_0_.2), channel_id=1, source_target_pairs={{0,4},{4,0},{8,12},{12,8},{16,20},{20,16},{24,28},{28,24},{1,5},{5... | collective-permute-start | bytes 196616 | tf_op jit(solution)/shard_map/ppermute | solution.py:19
  8.0 0.0 collective-permute-done.1.refs_2_
  8.0 0.3 collective-permute-start.2
  8.3 2.9 %collective-permute-done.3.refs_4_ = bf16[128,256]{1,0:T(8,128)(2,1)S(1)} collective-permute-done((bf16[128,256]{1,0:T(8,128)(2,1)}, bf16[128,256]{1,0:T(8,128)(2,1)S(1)}, u32[]{:S(2)}, u32[]{:S(2)}) %collective-permute-start.3) | collective-permute-done | bytes 65568 | tf_op jit(solution)/shard_map/ppermute | solution.py:19
  11.2 1.5 %collective-permute-start.4 = (bf16[128,256]{1,0:T(8,128)(2,1)S(1)}, bf16[128,256]{1,0:T(8,128)(2,1)S(1)}, u32[]{:S(2)}, u32[]{:S(2)}) collective-permute-start(bf16[128,256]{1,0:T(8,128)(2,1)S(1)} %collective-permute-done.3.refs_4_), channel_id=1, source_target_pairs={{0,4},{4,0},{8,12},{12,8},{16,20},{20,16},{24,28},{28,24},{1,5},{5... | collective-permute-start | bytes 196616 | tf_op jit(solution)/shard_map/ppermute | solution.py:19
  12.7 0.0 collective-permute-done.5.refs_6_
  12.7 1.4 %collective-permute-start.6 = (bf16[128,256]{1,0:T(8,128)(2,1)S(1)}, bf16[128,256]{1,0:T(8,128)(2,1)S(1)}, u32[]{:S(2)}, u32[]{:S(2)}) collective-permute-start(bf16[128,256]{1,0:T(8,128)(2,1)S(1)} %collective-permute-done.5.refs_6_), channel_id=1, source_target_pairs={{0,4},{4,0},{8,12},{12,8},{16,20},{20,16},{24,28},{28,24},{1,5},{5... | collective-permute-start | bytes 196616 | tf_op jit(solution)/shard_map/ppermute | solution.py:19
  14.1 0.8 %copy.9.coords = s32[1,1,8,2]{3,2,1,0:T(8,128)S(1)} copy(s32[1,1,8,2]{2,3,1,0:T(2,128)} %param.10) | data formatting | bytes 128 | tf_op args[4]
  15.5 0.0 collective-permute-done.refs_1_
  15.5 0.0 collective-permute-done.2.refs_3_
  15.5 0.0 collective-permute-done.4.refs_5_
  15.5 1.4 %collective-permute-done.6.refs_7_ = bf16[128,256]{1,0:T(8,128)(2,1)S(1)} collective-permute-done((bf16[128,256]{1,0:T(8,128)(2,1)S(1)}, bf16[128,256]{1,0:T(8,128)(2,1)S(1)}, u32[]{:S(2)}, u32[]{:S(2)}) %collective-permute-start.6) | collective-permute-done | bytes 65568 | tf_op jit(solution)/shard_map/ppermute | solution.py:19
  17.0 0.9 %copy-done = bf16[1,1,8,128,128]{4,3,2,1,0:T(8,128)(2,1)S(1)} copy-done((bf16[1,1,8,128,128]{4,3,2,1,0:T(8,128)(2,1)S(1)}, bf16[1,1,8,128,128]{4,3,2,1,0:T(8,128)(2,1)}, u32[]{:S(2)}) %copy-start) | copy-done | bytes 262168
  17.9 0.8 %copy-done.3 = bf16[128,256]{1,0:T(8,128)(2,1)S(1)} copy-done((bf16[128,256]{1,0:T(8,128)(2,1)S(1)}, bf16[128,256]{1,0:T(8,128)(2,1)}, u32[]{:S(2)}) %copy-start.3) | copy-done | bytes 65560
  18.8 1.0 %shard_map.85 = (bf16[256,256]{1,0:T(8,128)(2,1)S(1)}, bf16[256,256]{1,0:T(8,128)(2,1)S(1)}) custom-call(s32[1,1,8,2]{3,2,1,0:T(8,128)S(1)} %copy.9.coords, s32[1,1]{1,0:T(1,128)S(6)} %copy.11.count, bf16[1,1,8,128,128]{4,3,2,1,0:T(8,128)(2,1)S(1)} %copy-done, bf16[128,256]{1,0:T(8,128)(2,1)S(1)} %copy-done.3, ...), custom_call_target="tpu_custom_call" | custom-call | tf_op jit(solution)/shard_map/pallas_call | solution.py:149
  19.8 0.1 collective-permute-start.7
  19.8 1.3 %collective-permute-done.7.b = bf16[256,256]{1,0:T(8,128)(2,1)S(1)} collective-permute-done((bf16[256,256]{1,0:T(8,128)(2,1)S(1)}, bf16[256,256]{1,0:T(8,128)(2,1)S(1)}, u32[]{:S(2)}, u32[]{:S(2)}) %collective-permute-start.7) | collective-permute-done | bytes 131104 | tf_op jit(solution)/shard_map/ppermute | solution.py:19
  21.2 0.0 copy-start.1
  21.2 1.9 %collective-permute-start.8 = (bf16[256,256]{1,0:T(8,128)(2,1)S(1)}, bf16[256,256]{1,0:T(8,128)(2,1)S(1)}, u32[]{:S(2)}, u32[]{:S(2)}) collective-permute-start(bf16[256,256]{1,0:T(8,128)(2,1)S(1)} %shard_map.86.half), channel_id=1, source_target_pairs={{0,2},{1,3},{2,0},{3,1},{4,6},{5,7},{6,4},{7,5},{8,10},{9,11},{10,... | collective-permute-start | bytes 393224 | tf_op jit(solution)/shard_map/ppermute | solution.py:19
  23.1 0.7 %collective-permute-start.9 = (bf16[128,256]{1,0:T(8,128)(2,1)S(1)}, bf16[128,256]{1,0:T(8,128)(2,1)S(1)}, u32[]{:S(2)}, u32[]{:S(2)}) collective-permute-start(bf16[128,256]{1,0:T(8,128)(2,1)S(1)} %copy-done.4), channel_id=1, source_target_pairs={{0,2},{1,3},{2,0},{3,1},{4,6},{5,7},{6,4},{7,5},{8,10},{9,11},{10,... | collective-permute-start | bytes 196616 | tf_op jit(solution)/shard_map/ppermute | solution.py:19
  23.8 4.5 %collective-permute-done.9.refs_1_ = bf16[128,256]{1,0:T(8,128)(2,1)S(1)} collective-permute-done((bf16[128,256]{1,0:T(8,128)(2,1)S(1)}, bf16[128,256]{1,0:T(8,128)(2,1)S(1)}, u32[]{:S(2)}, u32[]{:S(2)}) %collective-permute-start.9) | collective-permute-done | bytes 65568 | tf_op jit(solution)/shard_map/ppermute | solution.py:19
  28.3 0.0 collective-permute-done.8.other
  28.3 1.1 %shard_map.87 = (bf16[128,256]{1,0:T(8,128)(2,1)}, bf16[320,256]{1,0:T(8,128)(2,1)S(1)}, bf16[64,256]{1,0:T(8,128)(2,1)S(1)}) custom-call(bf16[256,256]{1,0:T(8,128)(2,1)S(1)} %shard_map.86.half, bf16[256,256]{1,0:T(8,128)(2,1)S(1)} %collective-permute-done.8.other, bf16[256,256]{1,0:T(8,128)(2,1)S(1)} %copy-done.2, bf16[128,256]{1,0:T(8,128)(2,1)S(1)} %copy-done.4, ...), custom_call_target="tpu_custom_call" | custom-call | tf_op jit(solution)/shard_map/pallas_call | solution.py:168
  29.4 1.4 %collective-permute-done.10.other = bf16[320,256]{1,0:T(8,128)(2,1)S(1)} collective-permute-done((bf16[320,256]{1,0:T(8,128)(2,1)S(1)}, bf16[320,256]{1,0:T(8,128)(2,1)S(1)}, u32[]{:S(2)}, u32[]{:S(2)}) %collective-permute-start.10) | collective-permute-done | bytes 163872 | tf_op jit(solution)/shard_map/ppermute | solution.py:19
  30.8 1.1 %shard_map.92 = (bf16[512,256]{1,0:T(8,128)(2,1)S(1)}, bf16[512,256]{1,0:T(8,128)(2,1)S(1)}) custom-call(s32[1,1,8,2]{3,2,1,0:T(8,128)S(1)} %copy.9.coords, s32[1,1]{1,0:T(1,128)S(6)} %copy.11.count, bf16[1,1,8,128,128]{4,3,2,1,0:T(8,128)(2,1)S(1)} %copy-done.1, bf16[320,256]{1,0:T(8,128)(2,1)S(1)} %get-tuple-element.18.mine, ...), custom_call_target="tpu_custom_call" | custom-call | tf_op jit(solution)/shard_map/pallas_call | solution.py:176
  32.0 1.4 %collective-permute-start.18 = (bf16[512,256]{1,0:T(8,128)(2,1)S(1)}, bf16[512,256]{1,0:T(8,128)(2,1)S(1)}, u32[]{:S(2)}, u32[]{:S(2)}) collective-permute-start(bf16[512,256]{1,0:T(8,128)(2,1)S(1)} %get-tuple-element.20), channel_id=1, source_target_pairs={{0,4},{4,0},{8,12},{12,8},{16,20},{20,16},{24,28},{28,24},{1,5},{5... | collective-permute-start | bytes 786440 | tf_op jit(solution)/shard_map/ppermute | solution.py:19
  33.4 2.0 %collective-permute-start.11 = (bf16[64,256]{1,0:T(8,128)(2,1)S(1)}, bf16[64,256]{1,0:T(8,128)(2,1)S(1)}, u32[]{:S(2)}, u32[]{:S(2)}) collective-permute-start(bf16[64,256]{1,0:T(8,128)(2,1)S(1)} %shard_map.88.refs_0_), channel_id=1, source_target_pairs={{0,8},{4,12},{8,0},{12,4},{16,24},{20,28},{24,16},{28,20},{1,9},{5... | collective-permute-start | bytes 98312 | tf_op jit(solution)/shard_map/ppermute | solution.py:19
  35.4 1.7 %collective-permute-start.12 = (bf16[64,256]{1,0:T(8,128)(2,1)S(1)}, bf16[64,256]{1,0:T(8,128)(2,1)S(1)}, u32[]{:S(2)}, u32[]{:S(2)}) collective-permute-start(bf16[64,256]{1,0:T(8,128)(2,1)S(1)} %shard_map.88.refs_0_), channel_id=1, source_target_pairs={{0,16},{4,20},{8,24},{12,28},{16,0},{20,4},{24,8},{28,12},{1,17},{... | collective-permute-start | bytes 98312 | tf_op jit(solution)/shard_map/ppermute | solution.py:19
  37.2 0.7 %collective-permute-start.13 = (bf16[64,256]{1,0:T(8,128)(2,1)S(1)}, bf16[64,256]{1,0:T(8,128)(2,1)S(1)}, u32[]{:S(2)}, u32[]{:S(2)}) collective-permute-start(bf16[64,256]{1,0:T(8,128)(2,1)S(1)} %shard_map.88.refs_0_), channel_id=1, source_target_pairs={{0,24},{4,28},{8,16},{12,20},{16,8},{20,12},{24,0},{28,4},{1,25},{... | collective-permute-start | bytes 98312 | tf_op jit(solution)/shard_map/ppermute | solution.py:19
  37.9 2.4 %collective-permute-done.12.refs_2_ = bf16[64,256]{1,0:T(8,128)(2,1)S(1)} collective-permute-done((bf16[64,256]{1,0:T(8,128)(2,1)S(1)}, bf16[64,256]{1,0:T(8,128)(2,1)S(1)}, u32[]{:S(2)}, u32[]{:S(2)}) %collective-permute-start.12) | collective-permute-done | bytes 32800 | tf_op jit(solution)/shard_map/ppermute | solution.py:19
  40.2 2.6 %collective-permute-done.13.refs_3_ = bf16[64,256]{1,0:T(8,128)(2,1)S(1)} collective-permute-done((bf16[64,256]{1,0:T(8,128)(2,1)S(1)}, bf16[64,256]{1,0:T(8,128)(2,1)S(1)}, u32[]{:S(2)}, u32[]{:S(2)}) %collective-permute-start.13) | collective-permute-done | bytes 32800 | tf_op jit(solution)/shard_map/ppermute | solution.py:19
  42.9 1.4 %collective-permute-start.14 = (bf16[64,256]{1,0:T(8,128)(2,1)S(1)}, bf16[64,256]{1,0:T(8,128)(2,1)S(1)}, u32[]{:S(2)}, u32[]{:S(2)}) collective-permute-start(bf16[64,256]{1,0:T(8,128)(2,1)S(1)} %shard_map.89.refs_0_), channel_id=1, source_target_pairs={{0,4},{4,0},{8,12},{12,8},{16,20},{20,16},{24,28},{28,24},{1,5},{5... | collective-permute-start | bytes 98312 | tf_op jit(solution)/shard_map/ppermute | solution.py:19
  44.3 2.6 %collective-permute-done.14.refs_1_ = bf16[64,256]{1,0:T(8,128)(2,1)S(1)} collective-permute-done((bf16[64,256]{1,0:T(8,128)(2,1)S(1)}, bf16[64,256]{1,0:T(8,128)(2,1)S(1)}, u32[]{:S(2)}, u32[]{:S(2)}) %collective-permute-start.14) | collective-permute-done | bytes 32800 | tf_op jit(solution)/shard_map/ppermute | solution.py:19
  46.9 0.1 collective-permute-start.15
  47.0 0.1 shard_map.93
  47.1 0.1 collective-permute-start.19
  47.1 1.3 %collective-permute-start.20 = (bf16[128,256]{1,0:T(8,128)(2,1)S(1)}, bf16[128,256]{1,0:T(8,128)(2,1)S(1)}, u32[]{:S(2)}, u32[]{:S(2)}) collective-permute-start(bf16[128,256]{1,0:T(8,128)(2,1)S(1)} %get-tuple-element.23), channel_id=1, source_target_pairs={{0,16},{4,20},{8,24},{12,28},{16,0},{20,4},{24,8},{28,12},{1,17},{... | collective-permute-start | bytes 196616 | tf_op jit(solution)/shard_map/ppermute | solution.py:19
  48.4 3.1 %collective-permute-start.21 = (bf16[128,256]{1,0:T(8,128)(2,1)S(1)}, bf16[128,256]{1,0:T(8,128)(2,1)S(1)}, u32[]{:S(2)}, u32[]{:S(2)}) collective-permute-start(bf16[128,256]{1,0:T(8,128)(2,1)S(1)} %get-tuple-element.24), channel_id=1, source_target_pairs={{0,24},{4,28},{8,16},{12,20},{16,8},{20,12},{24,0},{28,4},{1,25},{... | collective-permute-start | bytes 196616 | tf_op jit(solution)/shard_map/ppermute | solution.py:19
  51.5 0.8 %collective-permute-start.16 = (bf16[64,256]{1,0:T(8,128)(2,1)S(1)}, bf16[64,256]{1,0:T(8,128)(2,1)S(1)}, u32[]{:S(2)}, u32[]{:S(2)}) collective-permute-start(bf16[64,256]{1,0:T(8,128)(2,1)S(1)} %shard_map.90.refs_0_), channel_id=1, source_target_pairs={{0,2},{1,3},{2,0},{3,1},{4,6},{5,7},{6,4},{7,5},{8,10},{9,11},{10,... | collective-permute-start | bytes 98312 | tf_op jit(solution)/shard_map/ppermute | solution.py:19
  52.3 0.0 collective-permute-done.15.refs_1_
  52.3 0.2 collective-permute-start.17
  52.5 3.0 %collective-permute-done.16.refs_2_ = bf16[64,256]{1,0:T(8,128)(2,1)S(1)} collective-permute-done((bf16[64,256]{1,0:T(8,128)(2,1)S(1)}, bf16[64,256]{1,0:T(8,128)(2,1)S(1)}, u32[]{:S(2)}, u32[]{:S(2)}) %collective-permute-start.16) | collective-permute-done | bytes 32800 | tf_op jit(solution)/shard_map/ppermute | solution.py:19
  55.5 0.5 collective-permute-done.17.refs_3_
  56.0 0.7 %shard_map.91 = f32[256,256]{1,0:T(8,128)} custom-call(bf16[64,256]{1,0:T(8,128)(2,1)S(1)} %shard_map.90.refs_0_, bf16[64,256]{1,0:T(8,128)(2,1)S(1)} %collective-permute-done.15.refs_1_, bf16[64,256]{1,0:T(8,128)(2,1)S(1)} %collective-permute-done.16.refs_2_, bf16[64,256]{1,0:T(8,128)(2,1)S(1)} %collective-permute-done.17.refs_3_), custom_call_target="tpu_custom_call" | custom-call | tf_op jit(solution)/shard_map/pallas_call | solution.py:191
  56.7 0.7 %shard_map.94 = bf16[128,256]{1,0:T(8,128)(2,1)} custom-call(bf16[128,256]{1,0:T(8,128)(2,1)S(1)} %get-tuple-element.21.refs_0_, bf16[128,256]{1,0:T(8,128)(2,1)S(1)} %collective-permute-done.19.refs_1_, bf16[128,256]{1,0:T(8,128)(2,1)S(1)} %collective-permute-done.20.refs_2_, bf16[128,256]{1,0:T(8,128)(2,1)S(1)} %collective-permute-done.21.refs_3_), custom_call_target="tpu_custom_call" | custom-call | tf_op jit(solution)/shard_map/pallas_call | solution.py:185
  (18 shorter events, 0.1 us)
Async XLA Ops:
  0.6 7.4 %collective-permute-start.1 = (bf16[128,256]{1,0:T(8,128)(2,1)}, bf16[128,256]{1,0:T(8,128)(2,1)S(1)}, u32[]{:S(2)}, u32[]{:S(2)}) collective-permute-start(bf16[128,256]{1,0:T(8,128)(2,1)} %refs_0_.2), channel_id=1, source_target_pairs={{0,8},{4,12},{8,0},{12,4},{16,24},{20,28},{24,16},{28,20},{1,9},{5... | collective-permute-start | bytes 196616 | tf_op jit(solution)/shard_map/ppermute | solution.py:19
  3.7 7.5 %collective-permute-start.3 = (bf16[128,256]{1,0:T(8,128)(2,1)}, bf16[128,256]{1,0:T(8,128)(2,1)S(1)}, u32[]{:S(2)}, u32[]{:S(2)}) collective-permute-start(bf16[128,256]{1,0:T(8,128)(2,1)} %refs_0_.2), channel_id=1, source_target_pairs={{0,16},{4,20},{8,24},{12,28},{16,0},{20,4},{24,8},{28,12},{1,17},{... | collective-permute-start | bytes 196616 | tf_op jit(solution)/shard_map/ppermute | solution.py:19
  6.3 6.4 %collective-permute-start.5 = (bf16[128,256]{1,0:T(8,128)(2,1)}, bf16[128,256]{1,0:T(8,128)(2,1)S(1)}, u32[]{:S(2)}, u32[]{:S(2)}) collective-permute-start(bf16[128,256]{1,0:T(8,128)(2,1)} %refs_0_.2), channel_id=1, source_target_pairs={{0,24},{4,28},{8,16},{12,20},{16,8},{20,12},{24,0},{28,4},{1,25},{... | collective-permute-start | bytes 196616 | tf_op jit(solution)/shard_map/ppermute | solution.py:19
  6.3 9.2 %collective-permute-start = (bf16[128,256]{1,0:T(8,128)(2,1)}, bf16[128,256]{1,0:T(8,128)(2,1)S(1)}, u32[]{:S(2)}, u32[]{:S(2)}) collective-permute-start(bf16[128,256]{1,0:T(8,128)(2,1)} %refs_0_.2), channel_id=1, source_target_pairs={{0,4},{4,0},{8,12},{12,8},{16,20},{20,16},{24,28},{28,24},{1,5},{5... | collective-permute-start | bytes 196616 | tf_op jit(solution)/shard_map/ppermute | solution.py:19
  8.0 7.5 %collective-permute-start.2 = (bf16[128,256]{1,0:T(8,128)(2,1)S(1)}, bf16[128,256]{1,0:T(8,128)(2,1)S(1)}, u32[]{:S(2)}, u32[]{:S(2)}) collective-permute-start(bf16[128,256]{1,0:T(8,128)(2,1)S(1)} %collective-permute-done.1.refs_2_), channel_id=1, source_target_pairs={{0,4},{4,0},{8,12},{12,8},{16,20},{20,16},{24,28},{28,24},{1,5},{5... | collective-permute-start | bytes 196616 | tf_op jit(solution)/shard_map/ppermute | solution.py:19
  11.2 4.3 %collective-permute-start.4 = (bf16[128,256]{1,0:T(8,128)(2,1)S(1)}, bf16[128,256]{1,0:T(8,128)(2,1)S(1)}, u32[]{:S(2)}, u32[]{:S(2)}) collective-permute-start(bf16[128,256]{1,0:T(8,128)(2,1)S(1)} %collective-permute-done.3.refs_4_), channel_id=1, source_target_pairs={{0,4},{4,0},{8,12},{12,8},{16,20},{20,16},{24,28},{28,24},{1,5},{5... | collective-permute-start | bytes 196616 | tf_op jit(solution)/shard_map/ppermute | solution.py:19
  12.7 4.3 %collective-permute-start.6 = (bf16[128,256]{1,0:T(8,128)(2,1)S(1)}, bf16[128,256]{1,0:T(8,128)(2,1)S(1)}, u32[]{:S(2)}, u32[]{:S(2)}) collective-permute-start(bf16[128,256]{1,0:T(8,128)(2,1)S(1)} %collective-permute-done.5.refs_6_), channel_id=1, source_target_pairs={{0,4},{4,0},{8,12},{12,8},{16,20},{20,16},{24,28},{28,24},{1,5},{5... | collective-permute-start | bytes 196616 | tf_op jit(solution)/shard_map/ppermute | solution.py:19
  17.0 1.0 %copy-start = (bf16[1,1,8,128,128]{4,3,2,1,0:T(8,128)(2,1)S(1)}, bf16[1,1,8,128,128]{4,3,2,1,0:T(8,128)(2,1)}, u32[]{:S(2)}) copy-start(bf16[1,1,8,128,128]{4,3,2,1,0:T(8,128)(2,1)} %tiles.3) | copy-start | bytes 786436
  17.9 0.8 %copy-start.3 = (bf16[128,256]{1,0:T(8,128)(2,1)S(1)}, bf16[128,256]{1,0:T(8,128)(2,1)}, u32[]{:S(2)}) copy-start(bf16[128,256]{1,0:T(8,128)(2,1)} %refs_0_.2) | copy-start | bytes 196612
  19.8 1.4 %collective-permute-start.7 = (bf16[256,256]{1,0:T(8,128)(2,1)S(1)}, bf16[256,256]{1,0:T(8,128)(2,1)S(1)}, u32[]{:S(2)}, u32[]{:S(2)}) collective-permute-start(bf16[256,256]{1,0:T(8,128)(2,1)S(1)} %get-tuple-element.15), channel_id=1, source_target_pairs={{0,1},{1,0},{2,3},{3,2},{4,5},{5,4},{6,7},{7,6},{8,9},{9,8},{10,11... | collective-permute-start | bytes 393224 | tf_op jit(solution)/shard_map/ppermute | solution.py:19
  21.2 1.9 %copy-start.4 = (bf16[128,256]{1,0:T(8,128)(2,1)S(1)}, bf16[128,256]{1,0:T(8,128)(2,1)}, u32[]{:S(2)}) copy-start(bf16[128,256]{1,0:T(8,128)(2,1)} %refs_0_.3) | copy-start | bytes 196612
  21.2 7.2 %copy-start.2 = (bf16[256,256]{1,0:T(8,128)(2,1)S(1)}, bf16[256,256]{1,0:T(8,128)(2,1)}, u32[]{:S(2)}) copy-start(bf16[256,256]{1,0:T(8,128)(2,1)} %weight.1) | copy-start | bytes 393220
  21.2 9.6 %copy-start.1 = (bf16[1,1,8,128,128]{4,3,2,1,0:T(8,128)(2,1)S(1)}, bf16[1,1,8,128,128]{4,3,2,1,0:T(8,128)(2,1)}, u32[]{:S(2)}) copy-start(bf16[1,1,8,128,128]{4,3,2,1,0:T(8,128)(2,1)} %tiles.3) | copy-start | bytes 786436
  21.2 7.1 %collective-permute-start.8 = (bf16[256,256]{1,0:T(8,128)(2,1)S(1)}, bf16[256,256]{1,0:T(8,128)(2,1)S(1)}, u32[]{:S(2)}, u32[]{:S(2)}) collective-permute-start(bf16[256,256]{1,0:T(8,128)(2,1)S(1)} %shard_map.86.half), channel_id=1, source_target_pairs={{0,2},{1,3},{2,0},{3,1},{4,6},{5,7},{6,4},{7,5},{8,10},{9,11},{10,... | collective-permute-start | bytes 393224 | tf_op jit(solution)/shard_map/ppermute | solution.py:19
  23.1 5.2 %collective-permute-start.9 = (bf16[128,256]{1,0:T(8,128)(2,1)S(1)}, bf16[128,256]{1,0:T(8,128)(2,1)S(1)}, u32[]{:S(2)}, u32[]{:S(2)}) collective-permute-start(bf16[128,256]{1,0:T(8,128)(2,1)S(1)} %copy-done.4), channel_id=1, source_target_pairs={{0,2},{1,3},{2,0},{3,1},{4,6},{5,7},{6,4},{7,5},{8,10},{9,11},{10,... | collective-permute-start | bytes 196616 | tf_op jit(solution)/shard_map/ppermute | solution.py:19
  29.4 1.4 %collective-permute-start.10 = (bf16[320,256]{1,0:T(8,128)(2,1)S(1)}, bf16[320,256]{1,0:T(8,128)(2,1)S(1)}, u32[]{:S(2)}, u32[]{:S(2)}) collective-permute-start(bf16[320,256]{1,0:T(8,128)(2,1)S(1)} %get-tuple-element.18.mine), channel_id=1, source_target_pairs={{0,1},{1,0},{2,3},{3,2},{4,5},{5,4},{6,7},{7,6},{8,9},{9,8},{10,11... | collective-permute-start | bytes 491528 | tf_op jit(solution)/shard_map/ppermute | solution.py:19
  32.0 15.0 %collective-permute-start.18 = (bf16[512,256]{1,0:T(8,128)(2,1)S(1)}, bf16[512,256]{1,0:T(8,128)(2,1)S(1)}, u32[]{:S(2)}, u32[]{:S(2)}) collective-permute-start(bf16[512,256]{1,0:T(8,128)(2,1)S(1)} %get-tuple-element.20), channel_id=1, source_target_pairs={{0,4},{4,0},{8,12},{12,8},{16,20},{20,16},{24,28},{28,24},{1,5},{5... | collective-permute-start | bytes 786440 | tf_op jit(solution)/shard_map/ppermute | solution.py:19
  33.4 4.5 %collective-permute-start.11 = (bf16[64,256]{1,0:T(8,128)(2,1)S(1)}, bf16[64,256]{1,0:T(8,128)(2,1)S(1)}, u32[]{:S(2)}, u32[]{:S(2)}) collective-permute-start(bf16[64,256]{1,0:T(8,128)(2,1)S(1)} %shard_map.88.refs_0_), channel_id=1, source_target_pairs={{0,8},{4,12},{8,0},{12,4},{16,24},{20,28},{24,16},{28,20},{1,9},{5... | collective-permute-start | bytes 98312 | tf_op jit(solution)/shard_map/ppermute | solution.py:19
  35.4 4.8 %collective-permute-start.12 = (bf16[64,256]{1,0:T(8,128)(2,1)S(1)}, bf16[64,256]{1,0:T(8,128)(2,1)S(1)}, u32[]{:S(2)}, u32[]{:S(2)}) collective-permute-start(bf16[64,256]{1,0:T(8,128)(2,1)S(1)} %shard_map.88.refs_0_), channel_id=1, source_target_pairs={{0,16},{4,20},{8,24},{12,28},{16,0},{20,4},{24,8},{28,12},{1,17},{... | collective-permute-start | bytes 98312 | tf_op jit(solution)/shard_map/ppermute | solution.py:19
  37.2 5.7 %collective-permute-start.13 = (bf16[64,256]{1,0:T(8,128)(2,1)S(1)}, bf16[64,256]{1,0:T(8,128)(2,1)S(1)}, u32[]{:S(2)}, u32[]{:S(2)}) collective-permute-start(bf16[64,256]{1,0:T(8,128)(2,1)S(1)} %shard_map.88.refs_0_), channel_id=1, source_target_pairs={{0,24},{4,28},{8,16},{12,20},{16,8},{20,12},{24,0},{28,4},{1,25},{... | collective-permute-start | bytes 98312 | tf_op jit(solution)/shard_map/ppermute | solution.py:19
  42.9 4.0 %collective-permute-start.14 = (bf16[64,256]{1,0:T(8,128)(2,1)S(1)}, bf16[64,256]{1,0:T(8,128)(2,1)S(1)}, u32[]{:S(2)}, u32[]{:S(2)}) collective-permute-start(bf16[64,256]{1,0:T(8,128)(2,1)S(1)} %shard_map.89.refs_0_), channel_id=1, source_target_pairs={{0,4},{4,0},{8,12},{12,8},{16,20},{20,16},{24,28},{28,24},{1,5},{5... | collective-permute-start | bytes 98312 | tf_op jit(solution)/shard_map/ppermute | solution.py:19
  46.9 5.4 %collective-permute-start.15 = (bf16[64,256]{1,0:T(8,128)(2,1)S(1)}, bf16[64,256]{1,0:T(8,128)(2,1)S(1)}, u32[]{:S(2)}, u32[]{:S(2)}) collective-permute-start(bf16[64,256]{1,0:T(8,128)(2,1)S(1)} %shard_map.90.refs_0_), channel_id=1, source_target_pairs={{0,1},{1,0},{2,3},{3,2},{4,5},{5,4},{6,7},{7,6},{8,9},{9,8},{10,11... | collective-permute-start | bytes 98312 | tf_op jit(solution)/shard_map/ppermute | solution.py:19
  47.1 9.7 %collective-permute-start.19 = (bf16[128,256]{1,0:T(8,128)(2,1)S(1)}, bf16[128,256]{1,0:T(8,128)(2,1)S(1)}, u32[]{:S(2)}, u32[]{:S(2)}) collective-permute-start(bf16[128,256]{1,0:T(8,128)(2,1)S(1)} %get-tuple-element.22), channel_id=1, source_target_pairs={{0,8},{4,12},{8,0},{12,4},{16,24},{20,28},{24,16},{28,20},{1,9},{5... | collective-permute-start | bytes 196616 | tf_op jit(solution)/shard_map/ppermute | solution.py:19
  47.1 9.6 %collective-permute-start.20 = (bf16[128,256]{1,0:T(8,128)(2,1)S(1)}, bf16[128,256]{1,0:T(8,128)(2,1)S(1)}, u32[]{:S(2)}, u32[]{:S(2)}) collective-permute-start(bf16[128,256]{1,0:T(8,128)(2,1)S(1)} %get-tuple-element.23), channel_id=1, source_target_pairs={{0,16},{4,20},{8,24},{12,28},{16,0},{20,4},{24,8},{28,12},{1,17},{... | collective-permute-start | bytes 196616 | tf_op jit(solution)/shard_map/ppermute | solution.py:19
  48.4 8.4 %collective-permute-start.21 = (bf16[128,256]{1,0:T(8,128)(2,1)S(1)}, bf16[128,256]{1,0:T(8,128)(2,1)S(1)}, u32[]{:S(2)}, u32[]{:S(2)}) collective-permute-start(bf16[128,256]{1,0:T(8,128)(2,1)S(1)} %get-tuple-element.24), channel_id=1, source_target_pairs={{0,24},{4,28},{8,16},{12,20},{16,8},{20,12},{24,0},{28,4},{1,25},{... | collective-permute-start | bytes 196616 | tf_op jit(solution)/shard_map/ppermute | solution.py:19
  51.5 4.0 %collective-permute-start.16 = (bf16[64,256]{1,0:T(8,128)(2,1)S(1)}, bf16[64,256]{1,0:T(8,128)(2,1)S(1)}, u32[]{:S(2)}, u32[]{:S(2)}) collective-permute-start(bf16[64,256]{1,0:T(8,128)(2,1)S(1)} %shard_map.90.refs_0_), channel_id=1, source_target_pairs={{0,2},{1,3},{2,0},{3,1},{4,6},{5,7},{6,4},{7,5},{8,10},{9,11},{10,... | collective-permute-start | bytes 98312 | tf_op jit(solution)/shard_map/ppermute | solution.py:19
  52.3 3.7 %collective-permute-start.17 = (bf16[64,256]{1,0:T(8,128)(2,1)S(1)}, bf16[64,256]{1,0:T(8,128)(2,1)S(1)}, u32[]{:S(2)}, u32[]{:S(2)}) collective-permute-start(bf16[64,256]{1,0:T(8,128)(2,1)S(1)} %shard_map.90.refs_0_), channel_id=1, source_target_pairs={{0,3},{1,2},{2,1},{3,0},{4,7},{5,6},{6,5},{7,4},{8,11},{9,10},{10,... | collective-permute-start | bytes 98312 | tf_op jit(solution)/shard_map/ppermute | solution.py:19

commit v2 on v1

v2 whole, which is shorter than its diff:
```python
import functools

import jax
import jax.numpy as jnp
from jax import lax
from jax.experimental import pallas as pl
from jax.experimental.pallas import tpu as pltpu
from jax.sharding import PartitionSpec as P

F32 = jnp.float32
BF16 = jnp.bfloat16
ANY = pl.BlockSpec(memory_space=pl.ANY)
VMEM = pl.BlockSpec(memory_space=pltpu.VMEM)
SMEM = pl.BlockSpec(memory_space=pltpu.SMEM)
VMEM_LIMIT = 16 * 1024 * 1024
DENSE_LIMIT = 2 * 1024 * 1024
ORDER = lambda n: [0, 1, *range(n - 2, 1, -2)]


def swap(value, row_bits=0, col_bits=0):
    n_row, n_col = lax.axis_size("row"), lax.axis_size("col")
    if not col_bits:
        return lax.ppermute(value, "row", [(i, i ^ row_bits) for i in range(n_row)])
    if not row_bits:
        return lax.ppermute(value, "col", [(j, j ^ col_bits) for j in range(n_col)])
    pairs = [
        (i * n_col + j, (i ^ row_bits) * n_col + (j ^ col_bits)) for i in range(n_row) for j in range(n_col)
    ]
    return lax.ppermute(value, ("row", "col"), pairs)


def call(kernel, outs, in_specs, scratch=(), out_spec=VMEM, us=0.0):
    return pl.pallas_call(
        kernel,
        out_shape=outs,
        in_specs=in_specs,
        out_specs=jax.tree.map(lambda _: out_spec, outs),
        scratch_shapes=list(scratch),
        compiler_params=pltpu.CompilerParams(vmem_limit_bytes=VMEM_LIMIT),
        cost_estimate=pl.CostEstimate(flops=0, bytes_accessed=int(us * 3.69e6), transcendentals=0) if us else None,
    )


def shape(rows, width, dtype=BF16):
    return jax.ShapeDtypeStruct((rows, width), dtype)


def block(ref, k, tile):
    return ref[k * tile:(k + 1) * tile, :]


def place_tiles(coords, count, tiles, *refs, tile, flipped):
    out = refs[-1]
    row, col = lax.axis_index("row"), lax.axis_index("col")
    out[...] = jnp.zeros_like(out)

    def step(s, carry):
        r = pl.multiple_of((coords[0, s] ^ col) * tile, tile)
        c = pl.multiple_of((coords[1, s] ^ row) * tile, tile)
        if flipped:
            out[pl.ds(c, tile), pl.ds(r, tile)] = tiles[0, 0, s].T
        else:
            out[pl.ds(r, tile), pl.ds(c, tile)] = tiles[0, 0, s]
        return carry

    lax.fori_loop(0, count[0, 0], step, 0)


def tile_loop(coords, count, tiles, source, total, flipped, tile):
    row, col = lax.axis_index("row"), lax.axis_index("col")
    total[...] = jnp.zeros_like(total)

    def step(s, carry):
        r = pl.multiple_of((coords[0, s] ^ col) * tile, tile)
        c = pl.multiple_of((coords[1, s] ^ row) * tile, tile)
        if flipped:
            total[pl.ds(c, tile), :] += lax.dot_general(
                tiles[0, 0, s], source[pl.ds(r, tile), :], (((0,), (0,)), ((), ())),
                preferred_element_type=F32,
            )
        else:
            total[pl.ds(r, tile), :] += jnp.dot(
                tiles[0, 0, s], source[pl.ds(c, tile), :], preferred_element_type=F32
            )
        return carry

    lax.fori_loop(0, count[0, 0], step, 0)


def product(adjacency, source, total, flipped, tile):
    if len(adjacency) == 1:
        total[...] = jnp.dot(adjacency[0][...], source[...], preferred_element_type=F32)
    else:
        tile_loop(*adjacency, source, total, flipped, tile)


def split_parity(total, keep, send, tile):
    for k in range(total.shape[0] // (2 * tile)):
        keep[k * tile:(k + 1) * tile, :] = block(total, 2 * k, tile).astype(BF16)
        send[k * tile:(k + 1) * tile, :] = block(total, 2 * k + 1, tile).astype(BF16)


def forward_kernel(*refs, n_adj, slots, tile):
    adjacency, parts = refs[:n_adj], refs[n_adj:n_adj + len(slots)]
    keep, send, source, total = refs[-4:]
    for group, part in zip(slots, parts):
        for n, slot in enumerate(group):
            source[slot * tile:(slot + 1) * tile, :] = block(part, n, tile)
    product(adjacency, source, total, False, tile)
    split_parity(total, keep, send, tile)


def backward_kernel(*refs, n_adj, tile):
    adjacency, (mine, other, kept, keep, send, grad, source, total) = refs[:n_adj], refs[n_adj:]
    for k in range(source.shape[0] // (2 * tile)):
        source[2 * k * tile:(2 * k + 1) * tile, :] = block(mine, k, tile)
        source[(2 * k + 1) * tile:(2 * k + 2) * tile, :] = block(other, k, tile)
    product(adjacency, source, total, True, tile)
    split_parity(total, keep, send, tile)
    rest = source.shape[0] // 2
    grad[...] = (kept[...].astype(F32) + other[rest:, :].astype(F32)).astype(BF16)


def add_kernel(a, b, out, *, flip, tile):
    for k in range(out.shape[0] // tile):
        total = block(a, k, tile).astype(F32) + block(b, k ^ flip, tile).astype(F32)
        out[k * tile:(k + 1) * tile, :] = total.astype(BF16)


def sum_parts(refs):
    total = refs[0][...].astype(F32)
    for ref in refs[1:]:
        total += ref[...].astype(F32)
    return total


def sum_kernel(*refs):
    refs[-1][...] = sum_parts(refs[:-2]).astype(BF16)


def split_kernel(a, b, *outs, tile):
    for k, out in enumerate(outs):
        out[...] = (block(a, k, tile).astype(F32) + block(b, k, tile).astype(F32)).astype(BF16)


def copy_kernel(value, out):
    out[...] = value[...]


def dense_kernel(half, other, weight, *refs, flip, tile, share):
    cots, (act, out, kept, agg, gpre) = refs[:-5], refs[-5:]
    blocks = len(cots)
    add_kernel(half, other, agg, flip=flip, tile=tile)
    col = lax.axis_index("col")
    for k in range(blocks):
        rows = slice(k * tile, (k + 1) * tile)
        pre = jnp.dot(agg[rows, :], weight[...], preferred_element_type=F32)
        sig = jax.nn.sigmoid(pre)
        if k == 0:
            act[...] = (pre * sig).astype(BF16)
        gpre[rows, :] = (cots[k][...].astype(F32) * sig * (1.0 + pre * (1.0 - sig))).astype(BF16)
    grad = lax.dot_general(
        gpre[...], weight[...], (((1,), (1,)), ((), ())), preferred_element_type=F32
    )
    out[:blocks * tile, :] = grad.astype(BF16)
    full = lax.dot_general(
        agg[...], gpre[...], (((0,), (0,)), ((), ())), preferred_element_type=F32
    ).astype(BF16)
    core = col % 2

    @pl.when(core == 0)
    def _():
        kept[...] = full[:share, :]
        out[blocks * tile:, :] = full[share:, :]

    @pl.when(core == 1)
    def _():
        kept[...] = full[share:, :]
        out[blocks * tile:, :] = full[:share, :]


def finish_kernel(act, *refs):
    mine, other, parts = refs[:2], refs[2:4], refs[4:-6]
    act_out, weight_out, input_out, total, grad, sems = refs[-6:]
    core = lax.axis_index("col") % 2
    share = grad.shape[1]
    copies = [pltpu.make_async_copy(act, act_out, sems.at[0])]
    copies[0].start()
    for n, values in enumerate((mine, other)):
        grad[n] = sum_parts(values)
        start = pl.multiple_of((core ^ n) * share, share)
        copies.append(pltpu.make_async_copy(grad.at[n], weight_out.at[pl.ds(start, share), :], sems.at[1 + n]))
        copies[-1].start()
    total[...] = sum_parts(parts).astype(BF16)
    copies.append(pltpu.make_async_copy(total, input_out, sems.at[3]))
    copies[-1].start()
    for copy in copies:
        copy.wait()


def body(features, weight, cotangent, adjacency_tiles, tile_coords, tile_counts):
    tile, width = features.shape
    n_row, n_col = lax.axis_size("row"), lax.axis_size("col")
    half = n_col // 2
    share = weight.shape[0] // 2
    coords = jnp.swapaxes(tile_coords[0, 0], 0, 1)

    def total(values, dtype=BF16):
        return call(sum_kernel, shape(*values[0].shape, dtype), [VMEM] * len(values))(*values)

    parts = {0: features}
    for m in [n_row - 2, *range(2, n_row - 2, 2)]:
        parts[m] = swap(features, m)
        parts[m] = call(copy_kernel, shape(tile, width), [VMEM], us=1.0)(parts[m])
        parts[m + 1] = swap(parts[m], 1)
    parts[1] = swap(features, 1)
    order = list(parts)
    slots, parts = [(m,) for m in order], [parts[m] for m in order]

    dense = n_row * n_col * tile * tile * 2 <= DENSE_LIMIT

    def placed(flipped, *after):
        sides = (n_row, n_col) if flipped else (n_col, n_row)
        return call(
            functools.partial(place_tiles, tile=tile, flipped=flipped),
            shape(sides[0] * tile, sides[1] * tile),
            [SMEM, SMEM, VMEM, *[ANY] * len(after)],
        )(coords, tile_counts, adjacency_tiles, *after)

    ahead = back = (coords, tile_counts, adjacency_tiles)
    specs = [SMEM, SMEM, VMEM]
    if dense:
        ahead, back, specs = (placed(False),), (placed(True),), [VMEM]

    cots = [cotangent] + [swap(cotangent, 0, 2 * k) for k in range(1, half)]
    keep, send = call(
        functools.partial(forward_kernel, n_adj=len(specs), slots=slots, tile=tile),
        [shape(half * tile, width)] * 2,
        [*specs, *[VMEM] * len(parts), *[ANY] * (half - 1)],
        [pltpu.VMEM((n_row * tile, width), BF16), pltpu.VMEM((n_col * tile, width), F32)],
    )(*ahead, *parts, *cots[1:])
    other = swap(send, 0, 1)
    partial = call(
        functools.partial(add_kernel, flip=0, tile=tile), shape(half * tile, width), [VMEM] * 2
    )(keep, other)
    bit = 1
    while bit < half:
        other = swap(partial, 0, 2 * bit)
        if 2 * bit < half:
            partial = call(
                functools.partial(add_kernel, flip=bit, tile=tile), shape(half * tile, width), [VMEM] * 2
            )(partial, other)
        bit *= 2
    act, out, kept = call(
        functools.partial(dense_kernel, flip=half // 2, tile=tile, share=share),
        [shape(tile, width), shape(half * tile + share, width), shape(share, width)],
        [VMEM] * (3 + half),
        [pltpu.VMEM((half * tile, width), BF16)] * 2,
    )(partial, other, weight, *cots)
    other = swap(out, 0, 1)

    keep, send, grad = call(
        functools.partial(backward_kernel, n_adj=len(specs), tile=tile),
        [shape(n_row // 2 * tile, width)] * 2 + [shape(share, width)],
        [*specs, VMEM, VMEM, VMEM],
        [pltpu.VMEM((n_col * tile, width), BF16), pltpu.VMEM((n_row * tile, width), F32)],
    )(*back, out, other, kept)
    other = swap(send, 1)
    grads = [grad] + [swap(grad, m) for m in range(2, n_row, 2)]
    pieces = call(
        functools.partial(split_kernel, tile=tile), [shape(tile, width)] * (n_row // 2), [VMEM] * 2
    )(keep, other)
    arrived = [pieces[0]] + [swap(pieces[k], 2 * k) for k in range(n_row // 2 - 1, 0, -1)]
    grad = call(sum_kernel, shape(share, width), [VMEM] * len(grads) + [ANY])(
        *grads, arrived[-1]
    )
    grads = [grad, swap(grad, 1), swap(grad, 0, 1), swap(grad, 1, 1)]
    return call(
        finish_kernel,
        [shape(tile, width), shape(*weight.shape, F32), shape(tile, width)],
        [VMEM] * (1 + len(grads) + len(arrived)),
        [pltpu.VMEM((tile, width), BF16), pltpu.VMEM((2, share, width), F32), pltpu.SemaphoreType.DMA((4,))],
        ANY,
    )(act, *grads, *arrived)


def solution(mesh):
    return jax.shard_map(
        body,
        mesh=mesh,
        in_specs=(
            P(("row", "col"), None),
            P(),
            P(("row", "col"), None),
            P("row", "col", None, None, None),
            P("row", "col", None, None),
            P("row", "col"),
        ),
        out_specs=(P(("row", "col"), None), P(), P(("row", "col"), None)),
        check_vma=False,
    )
```

time: 58.5 us -> 45.8 us (0.78); the launches traced: 57.4 us -> 45.6 us
  waiting for transfers between devices: 22.7 us -> 14.6 us
  local copies, waits for them, and re-layouts: 2.56 us -> 0.68 us
  starting transfers between devices: 26.1 us -> 25.1 us
  Pallas kernels: 4.74 us -> 3.8 us
    ppermute x22 -> x21, waiting for transfers between devices: 22.7 us -> 14.6 us  [the longest x15 8.72 us: swap(): return lax.ppermute(value, 'row', [(i, i ^ row_bits) for i in range(n_row)])]
    unnamed x11 -> x10, local copies, waits for them, and re-layouts: 2.56 us -> 0.68 us
    ppermute x22 -> x21, starting transfers between devices: 26.1 us -> 25.1 us  [the longest x15 20.5 us: swap(): return lax.ppermute(value, 'row', [(i, i ^ row_bits) for i in range(n_row)])]
    pallas_call x1, Pallas kernels: 1.09 us -> 0.45 us  [body(): call(functools.partial(dense_kernel, flip=half // 2, tile=tile, share=sha...]
    pallas_call x7 -> x9, Pallas kernels: 3.56 us -> 3.26 us  [the longest x2 1.56 us: placed(): call(functools.partial(place_tiles, tile=tile, flipped=flipped), shape(si...]
  transfers between devices with their start and end apart: 22 -> 21, of which waited for: 10 -> 10; matrix products, arithmetic and copies ran while one was open for 1% -> 0% of each run, Pallas kernels for 1% -> 4%
where the time goes in v2:
time: 45.8 us; the launch traced here: 45.6 us
  starting transfers between devices  25.1 us (55%)
  waiting for transfers between devices  14.6 us (32%)
  Pallas kernels  3.8 us (8%)
  between operations  1.42 us (3%)
  local copies, waits for them, and re-layouts  0.68 us (1%)
    ppermute x15, starting transfers between devices, swap(): return lax.ppermute(value, 'row', [(i, i ^ row_bits) for i in range(n_row)])  20.5 us
    ppermute x15, waiting for transfers between devices, swap(): return lax.ppermute(value, 'row', [(i, i ^ row_bits) for i in range(n_row)])  8.72 us
    ppermute x5, waiting for transfers between devices, swap(): return lax.ppermute(value, 'col', [(j, j ^ col_bits) for j in range(n_col)])  5.9 us
    ppermute x5, starting transfers between devices, swap(): return lax.ppermute(value, 'col', [(j, j ^ col_bits) for j in range(n_col)])  3.25 us
    pallas_call x2, Pallas kernels, placed(): call(functools.partial(place_tiles, tile=tile, flipped=flipped), shape(si...  1.56 us
    ppermute x1, starting transfers between devices, swap(): return lax.ppermute(value, ('row', 'col'), pairs)  1.3 us
  transfers between devices with their start and end apart: 21, of which 10 were waited for; matrix products, arithmetic and copies ran while one was open for 0% of the time, Pallas kernels for 4%

profile of v2, /device:TPU:0, one launch (start us, length us, event | category | flops | bytes accessed | tf_op | source)
XLA Modules:
  0.0 45.6 jit_solution(955305860227483357)
XLA Ops:
  0.6 5.1 %collective-permute-start = (bf16[128,256]{1,0:T(8,128)(2,1)}, bf16[128,256]{1,0:T(8,128)(2,1)S(1)}, u32[]{:S(2)}, u32[]{:S(2)}) collective-permute-start(bf16[128,256]{1,0:T(8,128)(2,1)} %refs_1_.1), channel_id=1, source_target_pairs={{0,24},{4,28},{8,16},{12,20},{16,8},{20,12},{24,0},{28,4},{1,25},{... | collective-permute-start | bytes 196616 | tf_op jit(solution)/shard_map/ppermute | solution.py:23
  5.8 0.0 collective-permute-start.2
  5.8 0.6 %collective-permute-start.4 = (bf16[128,256]{1,0:T(8,128)(2,1)}, bf16[128,256]{1,0:T(8,128)(2,1)S(1)}, u32[]{:S(2)}, u32[]{:S(2)}) collective-permute-start(bf16[128,256]{1,0:T(8,128)(2,1)} %refs_1_.1), channel_id=1, source_target_pairs={{0,16},{4,20},{8,24},{12,28},{16,0},{20,4},{24,8},{28,12},{1,17},{... | collective-permute-start | bytes 196616 | tf_op jit(solution)/shard_map/ppermute | solution.py:23
  6.4 1.6 %collective-permute-start.6 = (bf16[128,256]{1,0:T(8,128)(2,1)}, bf16[128,256]{1,0:T(8,128)(2,1)S(1)}, u32[]{:S(2)}, u32[]{:S(2)}) collective-permute-start(bf16[128,256]{1,0:T(8,128)(2,1)} %refs_1_.1), channel_id=1, source_target_pairs={{0,4},{4,0},{8,12},{12,8},{16,20},{20,16},{24,28},{28,24},{1,5},{5... | collective-permute-start | bytes 196616 | tf_op jit(solution)/shard_map/ppermute | solution.py:23
  8.0 1.5 %collective-permute-start.7 = (bf16[128,256]{1,0:T(8,128)(2,1)}, bf16[128,256]{1,0:T(8,128)(2,1)S(1)}, u32[]{:S(2)}, u32[]{:S(2)}) collective-permute-start(bf16[128,256]{1,0:T(8,128)(2,1)} %refs_0_.1), channel_id=1, source_target_pairs={{0,2},{1,3},{2,0},{3,1},{4,6},{5,7},{6,4},{7,5},{8,10},{9,11},{10,... | collective-permute-start | bytes 196616 | tf_op jit(solution)/shard_map/ppermute | solution.py:25
  9.6 0.0 collective-permute-done.value
  9.6 0.8 %collective-permute-start.1 = (bf16[128,256]{1,0:T(8,128)(2,1)S(1)}, bf16[128,256]{1,0:T(8,128)(2,1)S(1)}, u32[]{:S(2)}, u32[]{:S(2)}) collective-permute-start(bf16[128,256]{1,0:T(8,128)(2,1)S(1)} %shard_map.86.refs_2_), channel_id=1, source_target_pairs={{0,4},{4,0},{8,12},{12,8},{16,20},{20,16},{24,28},{28,24},{1,5},{5... | collective-permute-start | bytes 196616 | tf_op jit(solution)/shard_map/ppermute | solution.py:23
  10.4 0.3 collective-permute-done.2.value
  10.6 1.6 %collective-permute-start.3 = (bf16[128,256]{1,0:T(8,128)(2,1)S(1)}, bf16[128,256]{1,0:T(8,128)(2,1)S(1)}, u32[]{:S(2)}, u32[]{:S(2)}) collective-permute-start(bf16[128,256]{1,0:T(8,128)(2,1)S(1)} %shard_map.87.refs_4_), channel_id=1, source_target_pairs={{0,4},{4,0},{8,12},{12,8},{16,20},{20,16},{24,28},{28,24},{1,5},{5... | collective-permute-start | bytes 196616 | tf_op jit(solution)/shard_map/ppermute | solution.py:23
  12.3 0.0 collective-permute-done.4.value
  12.3 0.8 %collective-permute-start.5 = (bf16[128,256]{1,0:T(8,128)(2,1)S(1)}, bf16[128,256]{1,0:T(8,128)(2,1)S(1)}, u32[]{:S(2)}, u32[]{:S(2)}) collective-permute-start(bf16[128,256]{1,0:T(8,128)(2,1)S(1)} %shard_map.88.refs_6_), channel_id=1, source_target_pairs={{0,4},{4,0},{8,12},{12,8},{16,20},{20,16},{24,28},{28,24},{1,5},{5... | collective-permute-start | bytes 196616 | tf_op jit(solution)/shard_map/ppermute | solution.py:23
  13.7 0.0 copy-start.4
  13.8 0.7 %copy-done.4 = s32[1,1,8,2]{2,3,1,0:T(2,128)S(1)} copy-done((s32[1,1,8,2]{2,3,1,0:T(2,128)S(1)}, s32[1,1,8,2]{2,3,1,0:T(2,128)}, u32[]{:S(2)}) %copy-start.4) | copy-done | bytes 88
  14.4 0.7 %shard_map.85.refs_0_ = bf16[512,1024]{1,0:T(8,128)(2,1)S(1)} custom-call(s32[2,8]{1,0:T(2,128)S(1)} %bitcast.3, s32[1,1]{1,0:T(1,128)S(6)} %copy.9.count, bf16[1,1,8,128,128]{4,3,2,1,0:T(8,128)(2,1)S(1)} %copy-done), custom_call_target="tpu_custom_call" | custom-call | tf_op jit(solution)/shard_map/pallas_call | solution.py:224
  15.1 0.0 collective-permute-done.6.refs_8_
  15.1 0.0 collective-permute-done.7.refs_9_.refs_1_
  15.1 0.0 collective-permute-done.1.refs_3_
  15.1 0.4 collective-permute-done.3.refs_5_
  15.6 1.0 %collective-permute-done.5.refs_7_ = bf16[128,256]{1,0:T(8,128)(2,1)S(1)} collective-permute-done((bf16[128,256]{1,0:T(8,128)(2,1)S(1)}, bf16[128,256]{1,0:T(8,128)(2,1)S(1)}, u32[]{:S(2)}, u32[]{:S(2)}) %collective-permute-start.5) | collective-permute-done | bytes 65568 | tf_op jit(solution)/shard_map/ppermute | solution.py:23
  16.6 0.4 shard_map.89
  17.0 0.1 collective-permute-start.8
  17.1 1.3 %collective-permute-done.8.b = bf16[256,256]{1,0:T(8,128)(2,1)S(1)} collective-permute-done((bf16[256,256]{1,0:T(8,128)(2,1)S(1)}, bf16[256,256]{1,0:T(8,128)(2,1)S(1)}, u32[]{:S(2)}, u32[]{:S(2)}) %collective-permute-start.8) | collective-permute-done | bytes 131104 | tf_op jit(solution)/shard_map/ppermute | solution.py:25
  18.5 1.6 %collective-permute-start.9 = (bf16[256,256]{1,0:T(8,128)(2,1)S(1)}, bf16[256,256]{1,0:T(8,128)(2,1)S(1)}, u32[]{:S(2)}, u32[]{:S(2)}) collective-permute-start(bf16[256,256]{1,0:T(8,128)(2,1)S(1)} %shard_map.90.half), channel_id=1, source_target_pairs={{0,2},{1,3},{2,0},{3,1},{4,6},{5,7},{6,4},{7,5},{8,10},{9,11},{10,... | collective-permute-start | bytes 393224 | tf_op jit(solution)/shard_map/ppermute | solution.py:25
  20.1 4.0 %collective-permute-done.9.other = bf16[256,256]{1,0:T(8,128)(2,1)S(1)} collective-permute-done((bf16[256,256]{1,0:T(8,128)(2,1)S(1)}, bf16[256,256]{1,0:T(8,128)(2,1)S(1)}, u32[]{:S(2)}, u32[]{:S(2)}) %collective-permute-start.9) | collective-permute-done | bytes 131104 | tf_op jit(solution)/shard_map/ppermute | solution.py:25
  24.1 0.4 shard_map.91
  24.6 0.1 collective-permute-start.10
  24.7 0.9 %shard_map.92.refs_0_ = bf16[1024,512]{1,0:T(8,128)(2,1)S(1)} custom-call(s32[2,8]{1,0:T(2,128)S(1)} %bitcast.4, s32[1,1]{1,0:T(1,128)S(6)} %copy.9.count, bf16[1,1,8,128,128]{4,3,2,1,0:T(8,128)(2,1)S(1)} %copy-done), custom_call_target="tpu_custom_call" | custom-call | tf_op jit(solution)/shard_map/pallas_call | solution.py:224
  25.6 0.5 %collective-permute-done.10.refs_2_ = bf16[384,256]{1,0:T(8,128)(2,1)S(1)} collective-permute-done((bf16[384,256]{1,0:T(8,128)(2,1)S(1)}, bf16[384,256]{1,0:T(8,128)(2,1)S(1)}, u32[]{:S(2)}, u32[]{:S(2)}) %collective-permute-start.10) | collective-permute-done | bytes 196640 | tf_op jit(solution)/shard_map/ppermute | solution.py:25
  26.1 0.4 shard_map.93
  26.5 0.9 %collective-permute-start.14 = (bf16[512,256]{1,0:T(8,128)(2,1)S(1)}, bf16[512,256]{1,0:T(8,128)(2,1)S(1)}, u32[]{:S(2)}, u32[]{:S(2)}) collective-permute-start(bf16[512,256]{1,0:T(8,128)(2,1)S(1)} %get-tuple-element.22), channel_id=1, source_target_pairs={{0,4},{4,0},{8,12},{12,8},{16,20},{20,16},{24,28},{28,24},{1,5},{5... | collective-permute-start | bytes 786440 | tf_op jit(solution)/shard_map/ppermute | solution.py:23
  27.4 1.5 %collective-permute-start.11 = (bf16[128,256]{1,0:T(8,128)(2,1)S(1)}, bf16[128,256]{1,0:T(8,128)(2,1)S(1)}, u32[]{:S(2)}, u32[]{:S(2)}) collective-permute-start(bf16[128,256]{1,0:T(8,128)(2,1)S(1)} %get-tuple-element.20.refs_0_), channel_id=1, source_target_pairs={{0,8},{4,12},{8,0},{12,4},{16,24},{20,28},{24,16},{28,20},{1,9},{5... | collective-permute-start | bytes 196616 | tf_op jit(solution)/shard_map/ppermute | solution.py:23
  28.9 2.3 %collective-permute-start.12 = (bf16[128,256]{1,0:T(8,128)(2,1)S(1)}, bf16[128,256]{1,0:T(8,128)(2,1)S(1)}, u32[]{:S(2)}, u32[]{:S(2)}) collective-permute-start(bf16[128,256]{1,0:T(8,128)(2,1)S(1)} %get-tuple-element.20.refs_0_), channel_id=1, source_target_pairs={{0,16},{4,20},{8,24},{12,28},{16,0},{20,4},{24,8},{28,12},{1,17},{... | collective-permute-start | bytes 196616 | tf_op jit(solution)/shard_map/ppermute | solution.py:23
  31.2 0.6 %collective-permute-start.13 = (bf16[128,256]{1,0:T(8,128)(2,1)S(1)}, bf16[128,256]{1,0:T(8,128)(2,1)S(1)}, u32[]{:S(2)}, u32[]{:S(2)}) collective-permute-start(bf16[128,256]{1,0:T(8,128)(2,1)S(1)} %get-tuple-element.20.refs_0_), channel_id=1, source_target_pairs={{0,24},{4,28},{8,16},{12,20},{16,8},{20,12},{24,0},{28,4},{1,25},{... | collective-permute-start | bytes 196616 | tf_op jit(solution)/shard_map/ppermute | solution.py:23
  31.8 3.1 %collective-permute-done.14.b = bf16[512,256]{1,0:T(8,128)(2,1)S(1)} collective-permute-done((bf16[512,256]{1,0:T(8,128)(2,1)S(1)}, bf16[512,256]{1,0:T(8,128)(2,1)S(1)}, u32[]{:S(2)}, u32[]{:S(2)}) %collective-permute-start.14) | collective-permute-done | bytes 262176 | tf_op jit(solution)/shard_map/ppermute | solution.py:23
  34.9 0.1 shard_map.94
  35.0 1.2 %collective-permute-start.15 = (bf16[128,256]{1,0:T(8,128)(2,1)S(1)}, bf16[128,256]{1,0:T(8,128)(2,1)S(1)}, u32[]{:S(2)}, u32[]{:S(2)}) collective-permute-start(bf16[128,256]{1,0:T(8,128)(2,1)S(1)} %get-tuple-element.23), channel_id=1, source_target_pairs={{0,8},{4,12},{8,0},{12,4},{16,24},{20,28},{24,16},{28,20},{1,9},{5... | collective-permute-start | bytes 196616 | tf_op jit(solution)/shard_map/ppermute | solution.py:23
  36.2 2.0 %collective-permute-start.19 = (bf16[128,256]{1,0:T(8,128)(2,1)S(1)}, bf16[128,256]{1,0:T(8,128)(2,1)S(1)}, u32[]{:S(2)}, u32[]{:S(2)}) collective-permute-start(bf16[128,256]{1,0:T(8,128)(2,1)S(1)} %get-tuple-element.25), channel_id=1, source_target_pairs={{0,24},{4,28},{8,16},{12,20},{16,8},{20,12},{24,0},{28,4},{1,25},{... | collective-permute-start | bytes 196616 | tf_op jit(solution)/shard_map/ppermute | solution.py:23
  38.2 0.0 collective-permute-done.11.refs_1_
  38.2 0.5 %collective-permute-start.20 = (bf16[128,256]{1,0:T(8,128)(2,1)S(1)}, bf16[128,256]{1,0:T(8,128)(2,1)S(1)}, u32[]{:S(2)}, u32[]{:S(2)}) collective-permute-start(bf16[128,256]{1,0:T(8,128)(2,1)S(1)} %get-tuple-element.26), channel_id=1, source_target_pairs={{0,16},{4,20},{8,24},{12,28},{16,0},{20,4},{24,8},{28,12},{1,17},{... | collective-permute-start | bytes 196616 | tf_op jit(solution)/shard_map/ppermute | solution.py:23
  38.7 0.0 collective-permute-done.12.refs_2_
  38.7 0.0 collective-permute-done.13.refs_3_
  38.7 0.6 %collective-permute-done.15.refs_4_.refs_7_ = bf16[128,256]{1,0:T(8,128)(2,1)S(1)} collective-permute-done((bf16[128,256]{1,0:T(8,128)(2,1)S(1)}, bf16[128,256]{1,0:T(8,128)(2,1)S(1)}, u32[]{:S(2)}, u32[]{:S(2)}) %collective-permute-start.15) | collective-permute-done | bytes 65568 | tf_op jit(solution)/shard_map/ppermute | solution.py:23
  39.4 0.9 %collective-permute-start.16 = (bf16[128,256]{1,0:T(8,128)(2,1)S(1)}, bf16[128,256]{1,0:T(8,128)(2,1)S(1)}, u32[]{:S(2)}, u32[]{:S(2)}) collective-permute-start(bf16[128,256]{1,0:T(8,128)(2,1)S(1)} %shard_map.95.refs_0_), channel_id=1, source_target_pairs={{0,4},{4,0},{8,12},{12,8},{16,20},{20,16},{24,28},{28,24},{1,5},{5... | collective-permute-start | bytes 196616 | tf_op jit(solution)/shard_map/ppermute | solution.py:23
  40.3 0.0 collective-permute-start.17
  40.3 1.3 %collective-permute-start.18 = (bf16[128,256]{1,0:T(8,128)(2,1)S(1)}, bf16[128,256]{1,0:T(8,128)(2,1)S(1)}, u32[]{:S(2)}, u32[]{:S(2)}) collective-permute-start(bf16[128,256]{1,0:T(8,128)(2,1)S(1)} %shard_map.95.refs_0_), channel_id=1, source_target_pairs={{0,5},{1,4},{2,7},{3,6},{4,1},{5,0},{6,3},{7,2},{8,13},{9,12},{10,... | collective-permute-start | bytes 196616 | tf_op jit(solution)/shard_map/ppermute | solution.py:29
  41.6 1.0 %collective-permute-done.19.refs_5_ = bf16[128,256]{1,0:T(8,128)(2,1)S(1)} collective-permute-done((bf16[128,256]{1,0:T(8,128)(2,1)S(1)}, bf16[128,256]{1,0:T(8,128)(2,1)S(1)}, u32[]{:S(2)}, u32[]{:S(2)}) %collective-permute-start.19) | collective-permute-done | bytes 65568 | tf_op jit(solution)/shard_map/ppermute | solution.py:23
  42.5 2.3 %collective-permute-done.20.refs_6_ = bf16[128,256]{1,0:T(8,128)(2,1)S(1)} collective-permute-done((bf16[128,256]{1,0:T(8,128)(2,1)S(1)}, bf16[128,256]{1,0:T(8,128)(2,1)S(1)}, u32[]{:S(2)}, u32[]{:S(2)}) %collective-permute-start.20) | collective-permute-done | bytes 65568 | tf_op jit(solution)/shard_map/ppermute | solution.py:23
  44.8 0.8 %shard_map.96 = (bf16[128,256]{1,0:T(8,128)(2,1)}, f32[256,256]{1,0:T(8,128)}, bf16[128,256]{1,0:T(8,128)(2,1)}) custom-call(bf16[128,256]{1,0:T(8,128)(2,1)S(1)} %get-tuple-element.17.act, bf16[128,256]{1,0:T(8,128)(2,1)S(1)} %shard_map.95.refs_0_, bf16[128,256]{1,0:T(8,128)(2,1)S(1)} %collective-permute-done.16.refs_1_, ...), custom_call_target="tpu_custom_call" | custom-call | tf_op jit(solution)/shard_map/pallas_call | solution.py:278
  (16 shorter events, 0.1 us)
Async XLA Ops:
  0.6 13.1 %copy-start = (bf16[1,1,8,128,128]{4,3,2,1,0:T(8,128)(2,1)S(1)}, bf16[1,1,8,128,128]{4,3,2,1,0:T(8,128)(2,1)}, u32[]{:S(2)}) copy-start(bf16[1,1,8,128,128]{4,3,2,1,0:T(8,128)(2,1)} %tiles.3) | copy-start | bytes 786436
  0.6 8.9 %collective-permute-start = (bf16[128,256]{1,0:T(8,128)(2,1)}, bf16[128,256]{1,0:T(8,128)(2,1)S(1)}, u32[]{:S(2)}, u32[]{:S(2)}) collective-permute-start(bf16[128,256]{1,0:T(8,128)(2,1)} %refs_1_.1), channel_id=1, source_target_pairs={{0,24},{4,28},{8,16},{12,20},{16,8},{20,12},{24,0},{28,4},{1,25},{... | collective-permute-start | bytes 196616 | tf_op jit(solution)/shard_map/ppermute | solution.py:23
  5.8 4.9 %collective-permute-start.2 = (bf16[128,256]{1,0:T(8,128)(2,1)}, bf16[128,256]{1,0:T(8,128)(2,1)S(1)}, u32[]{:S(2)}, u32[]{:S(2)}) collective-permute-start(bf16[128,256]{1,0:T(8,128)(2,1)} %refs_1_.1), channel_id=1, source_target_pairs={{0,8},{4,12},{8,0},{12,4},{16,24},{20,28},{24,16},{28,20},{1,9},{5... | collective-permute-start | bytes 196616 | tf_op jit(solution)/shard_map/ppermute | solution.py:23
  5.8 6.5 %collective-permute-start.4 = (bf16[128,256]{1,0:T(8,128)(2,1)}, bf16[128,256]{1,0:T(8,128)(2,1)S(1)}, u32[]{:S(2)}, u32[]{:S(2)}) collective-permute-start(bf16[128,256]{1,0:T(8,128)(2,1)} %refs_1_.1), channel_id=1, source_target_pairs={{0,16},{4,20},{8,24},{12,28},{16,0},{20,4},{24,8},{28,12},{1,17},{... | collective-permute-start | bytes 196616 | tf_op jit(solution)/shard_map/ppermute | solution.py:23
  6.4 8.7 %collective-permute-start.6 = (bf16[128,256]{1,0:T(8,128)(2,1)}, bf16[128,256]{1,0:T(8,128)(2,1)S(1)}, u32[]{:S(2)}, u32[]{:S(2)}) collective-permute-start(bf16[128,256]{1,0:T(8,128)(2,1)} %refs_1_.1), channel_id=1, source_target_pairs={{0,4},{4,0},{8,12},{12,8},{16,20},{20,16},{24,28},{28,24},{1,5},{5... | collective-permute-start | bytes 196616 | tf_op jit(solution)/shard_map/ppermute | solution.py:23
  8.0 7.1 %collective-permute-start.7 = (bf16[128,256]{1,0:T(8,128)(2,1)}, bf16[128,256]{1,0:T(8,128)(2,1)S(1)}, u32[]{:S(2)}, u32[]{:S(2)}) collective-permute-start(bf16[128,256]{1,0:T(8,128)(2,1)} %refs_0_.1), channel_id=1, source_target_pairs={{0,2},{1,3},{2,0},{3,1},{4,6},{5,7},{6,4},{7,5},{8,10},{9,11},{10,... | collective-permute-start | bytes 196616 | tf_op jit(solution)/shard_map/ppermute | solution.py:25
  9.6 5.6 %collective-permute-start.1 = (bf16[128,256]{1,0:T(8,128)(2,1)S(1)}, bf16[128,256]{1,0:T(8,128)(2,1)S(1)}, u32[]{:S(2)}, u32[]{:S(2)}) collective-permute-start(bf16[128,256]{1,0:T(8,128)(2,1)S(1)} %shard_map.86.refs_2_), channel_id=1, source_target_pairs={{0,4},{4,0},{8,12},{12,8},{16,20},{20,16},{24,28},{28,24},{1,5},{5... | collective-permute-start | bytes 196616 | tf_op jit(solution)/shard_map/ppermute | solution.py:23
  10.6 4.9 %collective-permute-start.3 = (bf16[128,256]{1,0:T(8,128)(2,1)S(1)}, bf16[128,256]{1,0:T(8,128)(2,1)S(1)}, u32[]{:S(2)}, u32[]{:S(2)}) collective-permute-start(bf16[128,256]{1,0:T(8,128)(2,1)S(1)} %shard_map.87.refs_4_), channel_id=1, source_target_pairs={{0,4},{4,0},{8,12},{12,8},{16,20},{20,16},{24,28},{28,24},{1,5},{5... | collective-permute-start | bytes 196616 | tf_op jit(solution)/shard_map/ppermute | solution.py:23
  12.3 4.3 %collective-permute-start.5 = (bf16[128,256]{1,0:T(8,128)(2,1)S(1)}, bf16[128,256]{1,0:T(8,128)(2,1)S(1)}, u32[]{:S(2)}, u32[]{:S(2)}) collective-permute-start(bf16[128,256]{1,0:T(8,128)(2,1)S(1)} %shard_map.88.refs_6_), channel_id=1, source_target_pairs={{0,4},{4,0},{8,12},{12,8},{16,20},{20,16},{24,28},{28,24},{1,5},{5... | collective-permute-start | bytes 196616 | tf_op jit(solution)/shard_map/ppermute | solution.py:23
  13.7 0.7 %copy-start.4 = (s32[1,1,8,2]{2,3,1,0:T(2,128)S(1)}, s32[1,1,8,2]{2,3,1,0:T(2,128)}, u32[]{:S(2)}) copy-start(s32[1,1,8,2]{2,3,1,0:T(2,128)} %param.10) | copy-start | bytes 196
  14.4 2.2 %copy-start.2 = (bf16[128,256]{1,0:T(8,128)(2,1)S(1)}, bf16[128,256]{1,0:T(8,128)(2,1)}, u32[]{:S(2)}) copy-start(bf16[128,256]{1,0:T(8,128)(2,1)} %refs_1_.1) | copy-start | bytes 196612
  17.0 1.4 %collective-permute-start.8 = (bf16[256,256]{1,0:T(8,128)(2,1)S(1)}, bf16[256,256]{1,0:T(8,128)(2,1)S(1)}, u32[]{:S(2)}, u32[]{:S(2)}) collective-permute-start(bf16[256,256]{1,0:T(8,128)(2,1)S(1)} %get-tuple-element.16), channel_id=1, source_target_pairs={{0,1},{1,0},{2,3},{3,2},{4,5},{5,4},{6,7},{7,6},{8,9},{9,8},{10,11... | collective-permute-start | bytes 393224 | tf_op jit(solution)/shard_map/ppermute | solution.py:25
  18.5 5.7 %copy-start.1 = (bf16[256,256]{1,0:T(8,128)(2,1)S(1)}, bf16[256,256]{1,0:T(8,128)(2,1)}, u32[]{:S(2)}) copy-start(bf16[256,256]{1,0:T(8,128)(2,1)} %weight.1) | copy-start | bytes 393220
  18.5 5.7 %copy-start.3 = (bf16[128,256]{1,0:T(8,128)(2,1)S(1)}, bf16[128,256]{1,0:T(8,128)(2,1)}, u32[]{:S(2)}) copy-start(bf16[128,256]{1,0:T(8,128)(2,1)} %refs_0_.1) | copy-start | bytes 196612
  18.5 5.6 %collective-permute-start.9 = (bf16[256,256]{1,0:T(8,128)(2,1)S(1)}, bf16[256,256]{1,0:T(8,128)(2,1)S(1)}, u32[]{:S(2)}, u32[]{:S(2)}) collective-permute-start(bf16[256,256]{1,0:T(8,128)(2,1)S(1)} %shard_map.90.half), channel_id=1, source_target_pairs={{0,2},{1,3},{2,0},{3,1},{4,6},{5,7},{6,4},{7,5},{8,10},{9,11},{10,... | collective-permute-start | bytes 393224 | tf_op jit(solution)/shard_map/ppermute | solution.py:25
  24.6 1.5 %collective-permute-start.10 = (bf16[384,256]{1,0:T(8,128)(2,1)S(1)}, bf16[384,256]{1,0:T(8,128)(2,1)S(1)}, u32[]{:S(2)}, u32[]{:S(2)}) collective-permute-start(bf16[384,256]{1,0:T(8,128)(2,1)S(1)} %get-tuple-element.18.refs_1_), channel_id=1, source_target_pairs={{0,1},{1,0},{2,3},{3,2},{4,5},{5,4},{6,7},{7,6},{8,9},{9,8},{10,11... | collective-permute-start | bytes 589832 | tf_op jit(solution)/shard_map/ppermute | solution.py:25
  26.5 8.4 %collective-permute-start.14 = (bf16[512,256]{1,0:T(8,128)(2,1)S(1)}, bf16[512,256]{1,0:T(8,128)(2,1)S(1)}, u32[]{:S(2)}, u32[]{:S(2)}) collective-permute-start(bf16[512,256]{1,0:T(8,128)(2,1)S(1)} %get-tuple-element.22), channel_id=1, source_target_pairs={{0,4},{4,0},{8,12},{12,8},{16,20},{20,16},{24,28},{28,24},{1,5},{5... | collective-permute-start | bytes 786440 | tf_op jit(solution)/shard_map/ppermute | solution.py:23
  27.4 10.8 %collective-permute-start.11 = (bf16[128,256]{1,0:T(8,128)(2,1)S(1)}, bf16[128,256]{1,0:T(8,128)(2,1)S(1)}, u32[]{:S(2)}, u32[]{:S(2)}) collective-permute-start(bf16[128,256]{1,0:T(8,128)(2,1)S(1)} %get-tuple-element.20.refs_0_), channel_id=1, source_target_pairs={{0,8},{4,12},{8,0},{12,4},{16,24},{20,28},{24,16},{28,20},{1,9},{5... | collective-permute-start | bytes 196616 | tf_op jit(solution)/shard_map/ppermute | solution.py:23
  28.9 9.8 %collective-permute-start.12 = (bf16[128,256]{1,0:T(8,128)(2,1)S(1)}, bf16[128,256]{1,0:T(8,128)(2,1)S(1)}, u32[]{:S(2)}, u32[]{:S(2)}) collective-permute-start(bf16[128,256]{1,0:T(8,128)(2,1)S(1)} %get-tuple-element.20.refs_0_), channel_id=1, source_target_pairs={{0,16},{4,20},{8,24},{12,28},{16,0},{20,4},{24,8},{28,12},{1,17},{... | collective-permute-start | bytes 196616 | tf_op jit(solution)/shard_map/ppermute | solution.py:23
  31.2 7.5 %collective-permute-start.13 = (bf16[128,256]{1,0:T(8,128)(2,1)S(1)}, bf16[128,256]{1,0:T(8,128)(2,1)S(1)}, u32[]{:S(2)}, u32[]{:S(2)}) collective-permute-start(bf16[128,256]{1,0:T(8,128)(2,1)S(1)} %get-tuple-element.20.refs_0_), channel_id=1, source_target_pairs={{0,24},{4,28},{8,16},{12,20},{16,8},{20,12},{24,0},{28,4},{1,25},{... | collective-permute-start | bytes 196616 | tf_op jit(solution)/shard_map/ppermute | solution.py:23
  35.0 4.3 %collective-permute-start.15 = (bf16[128,256]{1,0:T(8,128)(2,1)S(1)}, bf16[128,256]{1,0:T(8,128)(2,1)S(1)}, u32[]{:S(2)}, u32[]{:S(2)}) collective-permute-start(bf16[128,256]{1,0:T(8,128)(2,1)S(1)} %get-tuple-element.23), channel_id=1, source_target_pairs={{0,8},{4,12},{8,0},{12,4},{16,24},{20,28},{24,16},{28,20},{1,9},{5... | collective-permute-start | bytes 196616 | tf_op jit(solution)/shard_map/ppermute | solution.py:23
  36.2 6.3 %collective-permute-start.19 = (bf16[128,256]{1,0:T(8,128)(2,1)S(1)}, bf16[128,256]{1,0:T(8,128)(2,1)S(1)}, u32[]{:S(2)}, u32[]{:S(2)}) collective-permute-start(bf16[128,256]{1,0:T(8,128)(2,1)S(1)} %get-tuple-element.25), channel_id=1, source_target_pairs={{0,24},{4,28},{8,16},{12,20},{16,8},{20,12},{24,0},{28,4},{1,25},{... | collective-permute-start | bytes 196616 | tf_op jit(solution)/shard_map/ppermute | solution.py:23
  38.2 6.6 %collective-permute-start.20 = (bf16[128,256]{1,0:T(8,128)(2,1)S(1)}, bf16[128,256]{1,0:T(8,128)(2,1)S(1)}, u32[]{:S(2)}, u32[]{:S(2)}) collective-permute-start(bf16[128,256]{1,0:T(8,128)(2,1)S(1)} %get-tuple-element.26), channel_id=1, source_target_pairs={{0,16},{4,20},{8,24},{12,28},{16,0},{20,4},{24,8},{28,12},{1,17},{... | collective-permute-start | bytes 196616 | tf_op jit(solution)/shard_map/ppermute | solution.py:23
  39.4 5.5 %collective-permute-start.16 = (bf16[128,256]{1,0:T(8,128)(2,1)S(1)}, bf16[128,256]{1,0:T(8,128)(2,1)S(1)}, u32[]{:S(2)}, u32[]{:S(2)}) collective-permute-start(bf16[128,256]{1,0:T(8,128)(2,1)S(1)} %shard_map.95.refs_0_), channel_id=1, source_target_pairs={{0,4},{4,0},{8,12},{12,8},{16,20},{20,16},{24,28},{28,24},{1,5},{5... | collective-permute-start | bytes 196616 | tf_op jit(solution)/shard_map/ppermute | solution.py:23
  40.3 4.6 %collective-permute-start.17 = (bf16[128,256]{1,0:T(8,128)(2,1)S(1)}, bf16[128,256]{1,0:T(8,128)(2,1)S(1)}, u32[]{:S(2)}, u32[]{:S(2)}) collective-permute-start(bf16[128,256]{1,0:T(8,128)(2,1)S(1)} %shard_map.95.refs_0_), channel_id=1, source_target_pairs={{0,1},{1,0},{2,3},{3,2},{4,5},{5,4},{6,7},{7,6},{8,9},{9,8},{10,11... | collective-permute-start | bytes 196616 | tf_op jit(solution)/shard_map/ppermute | solution.py:25
  40.3 4.6 %collective-permute-start.18 = (bf16[128,256]{1,0:T(8,128)(2,1)S(1)}, bf16[128,256]{1,0:T(8,128)(2,1)S(1)}, u32[]{:S(2)}, u32[]{:S(2)}) collective-permute-start(bf16[128,256]{1,0:T(8,128)(2,1)S(1)} %shard_map.95.refs_0_), channel_id=1, source_target_pairs={{0,5},{1,4},{2,7},{3,6},{4,1},{5,0},{6,3},{7,2},{8,13},{9,12},{10,... | collective-permute-start | bytes 196616 | tf_op jit(solution)/shard_map/ppermute | solution.py:29

commit v3 on v2

--- a/solution.py
+++ b/solution.py
@@ -14,7 +14,6 @@
 SMEM = pl.BlockSpec(memory_space=pltpu.SMEM)
 VMEM_LIMIT = 16 * 1024 * 1024
 DENSE_LIMIT = 2 * 1024 * 1024
-ORDER = lambda n: [0, 1, *range(n - 2, 1, -2)]
 
 
 def swap(value, row_bits=0, col_bits=0):
@@ -111,12 +110,14 @@
 
 
 def backward_kernel(*refs, n_adj, tile):
-    adjacency, (mine, other, kept, keep, send, grad, source, total) = refs[:n_adj], refs[n_adj:]
+    adjacency, (mine, other, kept, keep, keep_far, send, send_far, grad, source, total) = refs[:n_adj], refs[n_adj:]
     for k in range(source.shape[0] // (2 * tile)):
         source[2 * k * tile:(2 * k + 1) * tile, :] = block(mine, k, tile)
         source[(2 * k + 1) * tile:(2 * k + 2) * tile, :] = block(other, k, tile)
     product(adjacency, source, total, True, tile)
-    split_parity(total, keep, send, tile)
+    rows = total.shape[0] // 2
+    split_parity(total.at[rows:, :], keep_far, send_far, tile)
+    split_parity(total.at[:rows, :], keep, send, tile)
     rest = source.shape[0] // 2
     grad[...] = (kept[...].astype(F32) + other[rest:, :].astype(F32)).astype(BF16)
 
@@ -134,8 +135,8 @@
     return total
 
 
-def sum_kernel(*refs):
-    refs[-1][...] = sum_parts(refs[:-2]).astype(BF16)
+def sum_kernel(*refs, n):
+    refs[-1][...] = sum_parts(refs[:n]).astype(BF16)
 
 
 def split_kernel(a, b, *outs, tile):
@@ -205,9 +206,6 @@
     share = weight.shape[0] // 2
     coords = jnp.swapaxes(tile_coords[0, 0], 0, 1)
 
-    def total(values, dtype=BF16):
-        return call(sum_kernel, shape(*values[0].shape, dtype), [VMEM] * len(values))(*values)
-
     parts = {0: features}
     for m in [n_row - 2, *range(2, n_row - 2, 2)]:
         parts[m] = swap(features, m)
@@ -219,13 +217,13 @@
 
     dense = n_row * n_col * tile * tile * 2 <= DENSE_LIMIT
 
-    def placed(flipped, *after):
+    def placed(flipped):
         sides = (n_row, n_col) if flipped else (n_col, n_row)
         return call(
             functools.partial(place_tiles, tile=tile, flipped=flipped),
             shape(sides[0] * tile, sides[1] * tile),
-            [SMEM, SMEM, VMEM, *[ANY] * len(after)],
-        )(coords, tile_counts, adjacency_tiles, *after)
+            [SMEM, SMEM, VMEM],
+        )(coords, tile_counts, adjacency_tiles)
 
     ahead = back = (coords, tile_counts, adjacency_tiles)
     specs = [SMEM, SMEM, VMEM]
@@ -259,19 +257,22 @@
     )(partial, other, weight, *cots)
     other = swap(out, 0, 1)
 
-    keep, send, grad = call(
+    near, far, send, send_far, grad = call(
         functools.partial(backward_kernel, n_adj=len(specs), tile=tile),
-        [shape(n_row // 2 * tile, width)] * 2 + [shape(share, width)],
+        [shape(n_row // 4 * tile, width)] * 4 + [shape(share, width)],
         [*specs, VMEM, VMEM, VMEM],
         [pltpu.VMEM((n_col * tile, width), BF16), pltpu.VMEM((n_row * tile, width), F32)],
     )(*back, out, other, kept)
+    far_other = swap(send_far, 1)
     other = swap(send, 1)
     grads = [grad] + [swap(grad, m) for m in range(2, n_row, 2)]
-    pieces = call(
-        functools.partial(split_kernel, tile=tile), [shape(tile, width)] * (n_row // 2), [VMEM] * 2
-    )(keep, other)
-    arrived = [pieces[0]] + [swap(pieces[k], 2 * k) for k in range(n_row // 2 - 1, 0, -1)]
-    grad = call(sum_kernel, shape(share, width), [VMEM] * len(grads) + [ANY])(
+    halves = [
+        call(functools.partial(split_kernel, tile=tile), [shape(tile, width)] * (n_row // 4), [VMEM] * 2)(*pair)
+        for pair in ((near, other), (far, far_other))
+    ]
+    pieces = [*halves[0], *halves[1]]
+    arrived = [pieces[0]] + [swap(pieces[k], 2 * k) for k in [*range(2, n_row // 2), 1]]
+    grad = call(functools.partial(sum_kernel, n=len(grads)), shape(share, width), [VMEM] * len(grads) + [ANY])(
         *grads, arrived[-1]
     )
     grads = [grad, swap(grad, 1), swap(grad, 0, 1), swap(grad, 1, 1)]

time: 45.8 us -> 44.7 us (0.976)
  waiting for transfers between devices: 14.6 us -> 11.6 us
  starting transfers between devices: 25.1 us -> 27.3 us
    ppermute x15 -> x16, waiting for transfers between devices: 8.72 us -> 4.93 us  [swap(): return lax.ppermute(value, 'row', [(i, i ^ row_bits) for i in range(n_row)])]
    ppermute x15 -> x16, starting transfers between devices: 20.5 us -> 23.1 us  [swap(): return lax.ppermute(value, 'row', [(i, i ^ row_bits) for i in range(n_row)])]
    ppermute x1, waiting for transfers between devices: 0.01 us -> 0.58 us  [swap(): return lax.ppermute(value, ('row', 'col'), pairs)]
  transfers between devices with their start and end apart: 21 -> 22, of which waited for: 10 -> 9; matrix products, arithmetic and copies ran while one was open for 0% -> 0% of each run, Pallas kernels for 4% -> 3%
where the time goes in v3:
time: 44.7 us; the launch traced here: 44.6 us
  starting transfers between devices  27.3 us (61%)
  waiting for transfers between devices  11.6 us (26%)
  Pallas kernels  3.55 us (8%)
  between operations  1.43 us (3%)
  local copies, waits for them, and re-layouts  0.68 us (2%)
    ppermute x16, starting transfers between devices, swap(): return lax.ppermute(value, 'row', [(i, i ^ row_bits) for i in range(n_row)])  23.1 us
    ppermute x5, waiting for transfers between devices, swap(): return lax.ppermute(value, 'col', [(j, j ^ col_bits) for j in range(n_col)])  6.11 us
    ppermute x16, waiting for transfers between devices, swap(): return lax.ppermute(value, 'row', [(i, i ^ row_bits) for i in range(n_row)])  4.93 us
    ppermute x5, starting transfers between devices, swap(): return lax.ppermute(value, 'col', [(j, j ^ col_bits) for j in range(n_col)])  3.25 us
    pallas_call x2, Pallas kernels, placed(): call(functools.partial(place_tiles, tile=tile, flipped=flipped), shape(si...  1.31 us
    ppermute x1, starting transfers between devices, swap(): return lax.ppermute(value, ('row', 'col'), pairs)  0.97 us
  transfers between devices with their start and end apart: 22, of which 9 were waited for; matrix products, arithmetic and copies ran while one was open for 0% of the time, Pallas kernels for 3%

profile of v3, /device:TPU:0, one launch (start us, length us, event | category | flops | bytes accessed | tf_op | source)
XLA Modules:
  0.0 44.6 jit_solution(12567572156103487191)
XLA Ops:
  0.6 5.1 %collective-permute-start = (bf16[128,256]{1,0:T(8,128)(2,1)}, bf16[128,256]{1,0:T(8,128)(2,1)S(1)}, u32[]{:S(2)}, u32[]{:S(2)}) collective-permute-start(bf16[128,256]{1,0:T(8,128)(2,1)} %refs_1_.1), channel_id=1, source_target_pairs={{0,24},{4,28},{8,16},{12,20},{16,8},{20,12},{24,0},{28,4},{1,25},{... | collective-permute-start | bytes 196616 | tf_op jit(solution)/shard_map/ppermute | solution.py:22
  5.8 0.0 collective-permute-start.2
  5.8 0.6 %collective-permute-start.4 = (bf16[128,256]{1,0:T(8,128)(2,1)}, bf16[128,256]{1,0:T(8,128)(2,1)S(1)}, u32[]{:S(2)}, u32[]{:S(2)}) collective-permute-start(bf16[128,256]{1,0:T(8,128)(2,1)} %refs_1_.1), channel_id=1, source_target_pairs={{0,16},{4,20},{8,24},{12,28},{16,0},{20,4},{24,8},{28,12},{1,17},{... | collective-permute-start | bytes 196616 | tf_op jit(solution)/shard_map/ppermute | solution.py:22
  6.4 1.6 %collective-permute-start.6 = (bf16[128,256]{1,0:T(8,128)(2,1)}, bf16[128,256]{1,0:T(8,128)(2,1)S(1)}, u32[]{:S(2)}, u32[]{:S(2)}) collective-permute-start(bf16[128,256]{1,0:T(8,128)(2,1)} %refs_1_.1), channel_id=1, source_target_pairs={{0,4},{4,0},{8,12},{12,8},{16,20},{20,16},{24,28},{28,24},{1,5},{5... | collective-permute-start | bytes 196616 | tf_op jit(solution)/shard_map/ppermute | solution.py:22
  8.0 1.5 %collective-permute-start.7 = (bf16[128,256]{1,0:T(8,128)(2,1)}, bf16[128,256]{1,0:T(8,128)(2,1)S(1)}, u32[]{:S(2)}, u32[]{:S(2)}) collective-permute-start(bf16[128,256]{1,0:T(8,128)(2,1)} %refs_0_.1), channel_id=1, source_target_pairs={{0,2},{1,3},{2,0},{3,1},{4,6},{5,7},{6,4},{7,5},{8,10},{9,11},{10,... | collective-permute-start | bytes 196616 | tf_op jit(solution)/shard_map/ppermute | solution.py:24
  9.6 0.0 collective-permute-done.value
  9.6 0.8 %collective-permute-start.1 = (bf16[128,256]{1,0:T(8,128)(2,1)S(1)}, bf16[128,256]{1,0:T(8,128)(2,1)S(1)}, u32[]{:S(2)}, u32[]{:S(2)}) collective-permute-start(bf16[128,256]{1,0:T(8,128)(2,1)S(1)} %shard_map.86.refs_2_), channel_id=1, source_target_pairs={{0,4},{4,0},{8,12},{12,8},{16,20},{20,16},{24,28},{28,24},{1,5},{5... | collective-permute-start | bytes 196616 | tf_op jit(solution)/shard_map/ppermute | solution.py:22
  10.4 0.3 collective-permute-done.2.value
  10.6 1.6 %collective-permute-start.3 = (bf16[128,256]{1,0:T(8,128)(2,1)S(1)}, bf16[128,256]{1,0:T(8,128)(2,1)S(1)}, u32[]{:S(2)}, u32[]{:S(2)}) collective-permute-start(bf16[128,256]{1,0:T(8,128)(2,1)S(1)} %shard_map.87.refs_4_), channel_id=1, source_target_pairs={{0,4},{4,0},{8,12},{12,8},{16,20},{20,16},{24,28},{28,24},{1,5},{5... | collective-permute-start | bytes 196616 | tf_op jit(solution)/shard_map/ppermute | solution.py:22
  12.3 0.0 collective-permute-done.4.value
  12.3 0.8 %collective-permute-start.5 = (bf16[128,256]{1,0:T(8,128)(2,1)S(1)}, bf16[128,256]{1,0:T(8,128)(2,1)S(1)}, u32[]{:S(2)}, u32[]{:S(2)}) collective-permute-start(bf16[128,256]{1,0:T(8,128)(2,1)S(1)} %shard_map.88.refs_6_), channel_id=1, source_target_pairs={{0,4},{4,0},{8,12},{12,8},{16,20},{20,16},{24,28},{28,24},{1,5},{5... | collective-permute-start | bytes 196616 | tf_op jit(solution)/shard_map/ppermute | solution.py:22
  13.7 0.0 copy-start.4
  13.8 0.7 %copy-done.4 = s32[1,1,8,2]{2,3,1,0:T(2,128)S(1)} copy-done((s32[1,1,8,2]{2,3,1,0:T(2,128)S(1)}, s32[1,1,8,2]{2,3,1,0:T(2,128)}, u32[]{:S(2)}) %copy-start.4) | copy-done | bytes 88
  14.4 0.6 %shard_map.85.refs_0_ = bf16[512,1024]{1,0:T(8,128)(2,1)S(1)} custom-call(s32[2,8]{1,0:T(2,128)S(1)} %bitcast.3, s32[1,1]{1,0:T(1,128)S(6)} %copy.9.count, bf16[1,1,8,128,128]{4,3,2,1,0:T(8,128)(2,1)S(1)} %copy-done), custom_call_target="tpu_custom_call" | custom-call | tf_op jit(solution)/shard_map/pallas_call | solution.py:222
  15.1 0.0 collective-permute-done.6.refs_8_
  15.1 0.0 collective-permute-done.7.refs_9_.refs_1_
  15.1 0.0 collective-permute-done.1.refs_3_
  15.1 0.5 %collective-permute-done.3.refs_5_ = bf16[128,256]{1,0:T(8,128)(2,1)S(1)} collective-permute-done((bf16[128,256]{1,0:T(8,128)(2,1)S(1)}, bf16[128,256]{1,0:T(8,128)(2,1)S(1)}, u32[]{:S(2)}, u32[]{:S(2)}) %collective-permute-start.3) | collective-permute-done | bytes 65568 | tf_op jit(solution)/shard_map/ppermute | solution.py:22
  15.6 1.0 %collective-permute-done.5.refs_7_ = bf16[128,256]{1,0:T(8,128)(2,1)S(1)} collective-permute-done((bf16[128,256]{1,0:T(8,128)(2,1)S(1)}, bf16[128,256]{1,0:T(8,128)(2,1)S(1)}, u32[]{:S(2)}, u32[]{:S(2)}) %collective-permute-start.5) | collective-permute-done | bytes 65568 | tf_op jit(solution)/shard_map/ppermute | solution.py:22
  16.6 0.4 shard_map.89
  17.0 0.1 collective-permute-start.8
  17.1 1.3 %collective-permute-done.8.b = bf16[256,256]{1,0:T(8,128)(2,1)S(1)} collective-permute-done((bf16[256,256]{1,0:T(8,128)(2,1)S(1)}, bf16[256,256]{1,0:T(8,128)(2,1)S(1)}, u32[]{:S(2)}, u32[]{:S(2)}) %collective-permute-start.8) | collective-permute-done | bytes 131104 | tf_op jit(solution)/shard_map/ppermute | solution.py:24
  18.5 1.6 %collective-permute-start.9 = (bf16[256,256]{1,0:T(8,128)(2,1)S(1)}, bf16[256,256]{1,0:T(8,128)(2,1)S(1)}, u32[]{:S(2)}, u32[]{:S(2)}) collective-permute-start(bf16[256,256]{1,0:T(8,128)(2,1)S(1)} %shard_map.90.half), channel_id=1, source_target_pairs={{0,2},{1,3},{2,0},{3,1},{4,6},{5,7},{6,4},{7,5},{8,10},{9,11},{10,... | collective-permute-start | bytes 393224 | tf_op jit(solution)/shard_map/ppermute | solution.py:24
  20.1 4.0 %collective-permute-done.9.other = bf16[256,256]{1,0:T(8,128)(2,1)S(1)} collective-permute-done((bf16[256,256]{1,0:T(8,128)(2,1)S(1)}, bf16[256,256]{1,0:T(8,128)(2,1)S(1)}, u32[]{:S(2)}, u32[]{:S(2)}) %collective-permute-start.9) | collective-permute-done | bytes 131104 | tf_op jit(solution)/shard_map/ppermute | solution.py:24
  24.1 0.4 %shard_map.91 = (bf16[128,256]{1,0:T(8,128)(2,1)S(1)}, bf16[384,256]{1,0:T(8,128)(2,1)S(1)}, bf16[128,256]{1,0:T(8,128)(2,1)S(1)}) custom-call(bf16[256,256]{1,0:T(8,128)(2,1)S(1)} %shard_map.90.half, bf16[256,256]{1,0:T(8,128)(2,1)S(1)} %collective-permute-done.9.other, bf16[256,256]{1,0:T(8,128)(2,1)S(1)} %copy-done.1, bf16[128,256]{1,0:T(8,128)(2,1)S(1)} %copy-done.3, ...), custom_call_target="tpu_custom_call" | custom-call | tf_op jit(solution)/shard_map/pallas_call | solution.py:252
  24.6 0.1 collective-permute-start.10
  24.7 0.7 %shard_map.92.refs_0_ = bf16[1024,512]{1,0:T(8,128)(2,1)S(1)} custom-call(s32[2,8]{1,0:T(2,128)S(1)} %bitcast.4, s32[1,1]{1,0:T(1,128)S(6)} %copy.9.count, bf16[1,1,8,128,128]{4,3,2,1,0:T(8,128)(2,1)S(1)} %copy-done), custom_call_target="tpu_custom_call" | custom-call | tf_op jit(solution)/shard_map/pallas_call | solution.py:222
  25.3 0.7 %collective-permute-done.10.refs_2_ = bf16[384,256]{1,0:T(8,128)(2,1)S(1)} collective-permute-done((bf16[384,256]{1,0:T(8,128)(2,1)S(1)}, bf16[384,256]{1,0:T(8,128)(2,1)S(1)}, u32[]{:S(2)}, u32[]{:S(2)}) %collective-permute-start.10) | collective-permute-done | bytes 196640 | tf_op jit(solution)/shard_map/ppermute | solution.py:24
  26.1 0.4 shard_map.93
  26.5 0.9 %collective-permute-start.14 = (bf16[256,256]{1,0:T(8,128)(2,1)S(1)}, bf16[256,256]{1,0:T(8,128)(2,1)S(1)}, u32[]{:S(2)}, u32[]{:S(2)}) collective-permute-start(bf16[256,256]{1,0:T(8,128)(2,1)S(1)} %get-tuple-element.24), channel_id=1, source_target_pairs={{0,4},{4,0},{8,12},{12,8},{16,20},{20,16},{24,28},{28,24},{1,5},{5... | collective-permute-start | bytes 393224 | tf_op jit(solution)/shard_map/ppermute | solution.py:22
  27.4 1.2 %collective-permute-start.19 = (bf16[256,256]{1,0:T(8,128)(2,1)S(1)}, bf16[256,256]{1,0:T(8,128)(2,1)S(1)}, u32[]{:S(2)}, u32[]{:S(2)}) collective-permute-start(bf16[256,256]{1,0:T(8,128)(2,1)S(1)} %get-tuple-element.28), channel_id=1, source_target_pairs={{0,4},{4,0},{8,12},{12,8},{16,20},{20,16},{24,28},{28,24},{1,5},{5... | collective-permute-start | bytes 393224 | tf_op jit(solution)/shard_map/ppermute | solution.py:22
  28.6 1.1 %collective-permute-start.11 = (bf16[128,256]{1,0:T(8,128)(2,1)S(1)}, bf16[128,256]{1,0:T(8,128)(2,1)S(1)}, u32[]{:S(2)}, u32[]{:S(2)}) collective-permute-start(bf16[128,256]{1,0:T(8,128)(2,1)S(1)} %get-tuple-element.22.refs_0_), channel_id=1, source_target_pairs={{0,8},{4,12},{8,0},{12,4},{16,24},{20,28},{24,16},{28,20},{1,9},{5... | collective-permute-start | bytes 196616 | tf_op jit(solution)/shard_map/ppermute | solution.py:22
  29.8 2.5 %collective-permute-start.12 = (bf16[128,256]{1,0:T(8,128)(2,1)S(1)}, bf16[128,256]{1,0:T(8,128)(2,1)S(1)}, u32[]{:S(2)}, u32[]{:S(2)}) collective-permute-start(bf16[128,256]{1,0:T(8,128)(2,1)S(1)} %get-tuple-element.22.refs_0_), channel_id=1, source_target_pairs={{0,16},{4,20},{8,24},{12,28},{16,0},{20,4},{24,8},{28,12},{1,17},{... | collective-permute-start | bytes 196616 | tf_op jit(solution)/shard_map/ppermute | solution.py:22
  32.2 0.8 %collective-permute-start.13 = (bf16[128,256]{1,0:T(8,128)(2,1)S(1)}, bf16[128,256]{1,0:T(8,128)(2,1)S(1)}, u32[]{:S(2)}, u32[]{:S(2)}) collective-permute-start(bf16[128,256]{1,0:T(8,128)(2,1)S(1)} %get-tuple-element.22.refs_0_), channel_id=1, source_target_pairs={{0,24},{4,28},{8,16},{12,20},{16,8},{20,12},{24,0},{28,4},{1,25},{... | collective-permute-start | bytes 196616 | tf_op jit(solution)/shard_map/ppermute | solution.py:22
  33.0 0.0 collective-permute-done.14.b
  33.0 1.1 %collective-permute-start.15 = (bf16[128,256]{1,0:T(8,128)(2,1)S(1)}, bf16[128,256]{1,0:T(8,128)(2,1)S(1)}, u32[]{:S(2)}, u32[]{:S(2)}) collective-permute-start(bf16[128,256]{1,0:T(8,128)(2,1)S(1)} %get-tuple-element.25), channel_id=1, source_target_pairs={{0,8},{4,12},{8,0},{12,4},{16,24},{20,28},{24,16},{28,20},{1,9},{5... | collective-permute-start | bytes 196616 | tf_op jit(solution)/shard_map/ppermute | solution.py:22
  34.2 0.8 %collective-permute-done.19.b = bf16[256,256]{1,0:T(8,128)(2,1)S(1)} collective-permute-done((bf16[256,256]{1,0:T(8,128)(2,1)S(1)}, bf16[256,256]{1,0:T(8,128)(2,1)S(1)}, u32[]{:S(2)}, u32[]{:S(2)}) %collective-permute-start.19) | collective-permute-done | bytes 131104 | tf_op jit(solution)/shard_map/ppermute | solution.py:22
  35.0 1.9 %collective-permute-start.20 = (bf16[128,256]{1,0:T(8,128)(2,1)S(1)}, bf16[128,256]{1,0:T(8,128)(2,1)S(1)}, u32[]{:S(2)}, u32[]{:S(2)}) collective-permute-start(bf16[128,256]{1,0:T(8,128)(2,1)S(1)} %get-tuple-element.29), channel_id=1, source_target_pairs={{0,16},{4,20},{8,24},{12,28},{16,0},{20,4},{24,8},{28,12},{1,17},{... | collective-permute-start | bytes 196616 | tf_op jit(solution)/shard_map/ppermute | solution.py:22
  36.8 0.0 collective-permute-done.11.refs_1_
  36.8 1.7 %collective-permute-start.21 = (bf16[128,256]{1,0:T(8,128)(2,1)S(1)}, bf16[128,256]{1,0:T(8,128)(2,1)S(1)}, u32[]{:S(2)}, u32[]{:S(2)}) collective-permute-start(bf16[128,256]{1,0:T(8,128)(2,1)S(1)} %get-tuple-element.30), channel_id=1, source_target_pairs={{0,24},{4,28},{8,16},{12,20},{16,8},{20,12},{24,0},{28,4},{1,25},{... | collective-permute-start | bytes 196616 | tf_op jit(solution)/shard_map/ppermute | solution.py:22
  38.5 0.0 collective-permute-done.12.refs_2_
  38.6 1.2 %collective-permute-start.16 = (bf16[128,256]{1,0:T(8,128)(2,1)S(1)}, bf16[128,256]{1,0:T(8,128)(2,1)S(1)}, u32[]{:S(2)}, u32[]{:S(2)}) collective-permute-start(bf16[128,256]{1,0:T(8,128)(2,1)S(1)} %shard_map.95.refs_0_), channel_id=1, source_target_pairs={{0,4},{4,0},{8,12},{12,8},{16,20},{20,16},{24,28},{28,24},{1,5},{5... | collective-permute-start | bytes 196616 | tf_op jit(solution)/shard_map/ppermute | solution.py:22
  39.8 1.0 %collective-permute-start.18 = (bf16[128,256]{1,0:T(8,128)(2,1)S(1)}, bf16[128,256]{1,0:T(8,128)(2,1)S(1)}, u32[]{:S(2)}, u32[]{:S(2)}) collective-permute-start(bf16[128,256]{1,0:T(8,128)(2,1)S(1)} %shard_map.95.refs_0_), channel_id=1, source_target_pairs={{0,5},{1,4},{2,7},{3,6},{4,1},{5,0},{6,3},{7,2},{8,13},{9,12},{10,... | collective-permute-start | bytes 196616 | tf_op jit(solution)/shard_map/ppermute | solution.py:28
  40.8 2.4 %collective-permute-done.20.refs_5_ = bf16[128,256]{1,0:T(8,128)(2,1)S(1)} collective-permute-done((bf16[128,256]{1,0:T(8,128)(2,1)S(1)}, bf16[128,256]{1,0:T(8,128)(2,1)S(1)}, u32[]{:S(2)}, u32[]{:S(2)}) %collective-permute-start.20) | collective-permute-done | bytes 65568 | tf_op jit(solution)/shard_map/ppermute | solution.py:22
  43.2 0.0 collective-permute-done.21.refs_6_
  43.2 0.0 collective-permute-done.16.refs_1_
  43.2 0.6 %collective-permute-done.18.refs_3_ = bf16[128,256]{1,0:T(8,128)(2,1)S(1)} collective-permute-done((bf16[128,256]{1,0:T(8,128)(2,1)S(1)}, bf16[128,256]{1,0:T(8,128)(2,1)S(1)}, u32[]{:S(2)}, u32[]{:S(2)}) %collective-permute-start.18) | collective-permute-done | bytes 65568 | tf_op jit(solution)/shard_map/ppermute | solution.py:28
  43.8 0.8 %shard_map.97 = (bf16[128,256]{1,0:T(8,128)(2,1)}, f32[256,256]{1,0:T(8,128)}, bf16[128,256]{1,0:T(8,128)(2,1)}) custom-call(bf16[128,256]{1,0:T(8,128)(2,1)S(1)} %get-tuple-element.19.act, bf16[128,256]{1,0:T(8,128)(2,1)S(1)} %shard_map.95.refs_0_, bf16[128,256]{1,0:T(8,128)(2,1)S(1)} %collective-permute-done.16.refs_1_, ...), custom_call_target="tpu_custom_call" | custom-call | tf_op jit(solution)/shard_map/pallas_call | solution.py:279
  (19 shorter events, 0.2 us)
Async XLA Ops:
  0.6 13.1 %copy-start = (bf16[1,1,8,128,128]{4,3,2,1,0:T(8,128)(2,1)S(1)}, bf16[1,1,8,128,128]{4,3,2,1,0:T(8,128)(2,1)}, u32[]{:S(2)}) copy-start(bf16[1,1,8,128,128]{4,3,2,1,0:T(8,128)(2,1)} %tiles.3) | copy-start | bytes 786436
  0.6 8.9 %collective-permute-start = (bf16[128,256]{1,0:T(8,128)(2,1)}, bf16[128,256]{1,0:T(8,128)(2,1)S(1)}, u32[]{:S(2)}, u32[]{:S(2)}) collective-permute-start(bf16[128,256]{1,0:T(8,128)(2,1)} %refs_1_.1), channel_id=1, source_target_pairs={{0,24},{4,28},{8,16},{12,20},{16,8},{20,12},{24,0},{28,4},{1,25},{... | collective-permute-start | bytes 196616 | tf_op jit(solution)/shard_map/ppermute | solution.py:22
  5.8 4.9 %collective-permute-start.2 = (bf16[128,256]{1,0:T(8,128)(2,1)}, bf16[128,256]{1,0:T(8,128)(2,1)S(1)}, u32[]{:S(2)}, u32[]{:S(2)}) collective-permute-start(bf16[128,256]{1,0:T(8,128)(2,1)} %refs_1_.1), channel_id=1, source_target_pairs={{0,8},{4,12},{8,0},{12,4},{16,24},{20,28},{24,16},{28,20},{1,9},{5... | collective-permute-start | bytes 196616 | tf_op jit(solution)/shard_map/ppermute | solution.py:22
  5.8 6.5 %collective-permute-start.4 = (bf16[128,256]{1,0:T(8,128)(2,1)}, bf16[128,256]{1,0:T(8,128)(2,1)S(1)}, u32[]{:S(2)}, u32[]{:S(2)}) collective-permute-start(bf16[128,256]{1,0:T(8,128)(2,1)} %refs_1_.1), channel_id=1, source_target_pairs={{0,16},{4,20},{8,24},{12,28},{16,0},{20,4},{24,8},{28,12},{1,17},{... | collective-permute-start | bytes 196616 | tf_op jit(solution)/shard_map/ppermute | solution.py:22
  6.4 8.7 %collective-permute-start.6 = (bf16[128,256]{1,0:T(8,128)(2,1)}, bf16[128,256]{1,0:T(8,128)(2,1)S(1)}, u32[]{:S(2)}, u32[]{:S(2)}) collective-permute-start(bf16[128,256]{1,0:T(8,128)(2,1)} %refs_1_.1), channel_id=1, source_target_pairs={{0,4},{4,0},{8,12},{12,8},{16,20},{20,16},{24,28},{28,24},{1,5},{5... | collective-permute-start | bytes 196616 | tf_op jit(solution)/shard_map/ppermute | solution.py:22
  8.0 7.0 %collective-permute-start.7 = (bf16[128,256]{1,0:T(8,128)(2,1)}, bf16[128,256]{1,0:T(8,128)(2,1)S(1)}, u32[]{:S(2)}, u32[]{:S(2)}) collective-permute-start(bf16[128,256]{1,0:T(8,128)(2,1)} %refs_0_.1), channel_id=1, source_target_pairs={{0,2},{1,3},{2,0},{3,1},{4,6},{5,7},{6,4},{7,5},{8,10},{9,11},{10,... | collective-permute-start | bytes 196616 | tf_op jit(solution)/shard_map/ppermute | solution.py:24
  9.6 5.5 %collective-permute-start.1 = (bf16[128,256]{1,0:T(8,128)(2,1)S(1)}, bf16[128,256]{1,0:T(8,128)(2,1)S(1)}, u32[]{:S(2)}, u32[]{:S(2)}) collective-permute-start(bf16[128,256]{1,0:T(8,128)(2,1)S(1)} %shard_map.86.refs_2_), channel_id=1, source_target_pairs={{0,4},{4,0},{8,12},{12,8},{16,20},{20,16},{24,28},{28,24},{1,5},{5... | collective-permute-start | bytes 196616 | tf_op jit(solution)/shard_map/ppermute | solution.py:22
  10.6 4.9 %collective-permute-start.3 = (bf16[128,256]{1,0:T(8,128)(2,1)S(1)}, bf16[128,256]{1,0:T(8,128)(2,1)S(1)}, u32[]{:S(2)}, u32[]{:S(2)}) collective-permute-start(bf16[128,256]{1,0:T(8,128)(2,1)S(1)} %shard_map.87.refs_4_), channel_id=1, source_target_pairs={{0,4},{4,0},{8,12},{12,8},{16,20},{20,16},{24,28},{28,24},{1,5},{5... | collective-permute-start | bytes 196616 | tf_op jit(solution)/shard_map/ppermute | solution.py:22
  12.3 4.3 %collective-permute-start.5 = (bf16[128,256]{1,0:T(8,128)(2,1)S(1)}, bf16[128,256]{1,0:T(8,128)(2,1)S(1)}, u32[]{:S(2)}, u32[]{:S(2)}) collective-permute-start(bf16[128,256]{1,0:T(8,128)(2,1)S(1)} %shard_map.88.refs_6_), channel_id=1, source_target_pairs={{0,4},{4,0},{8,12},{12,8},{16,20},{20,16},{24,28},{28,24},{1,5},{5... | collective-permute-start | bytes 196616 | tf_op jit(solution)/shard_map/ppermute | solution.py:22
  13.7 0.7 %copy-start.4 = (s32[1,1,8,2]{2,3,1,0:T(2,128)S(1)}, s32[1,1,8,2]{2,3,1,0:T(2,128)}, u32[]{:S(2)}) copy-start(s32[1,1,8,2]{2,3,1,0:T(2,128)} %param.10) | copy-start | bytes 196
  14.4 2.2 %copy-start.2 = (bf16[128,256]{1,0:T(8,128)(2,1)S(1)}, bf16[128,256]{1,0:T(8,128)(2,1)}, u32[]{:S(2)}) copy-start(bf16[128,256]{1,0:T(8,128)(2,1)} %refs_1_.1) | copy-start | bytes 196612
  17.0 1.4 %collective-permute-start.8 = (bf16[256,256]{1,0:T(8,128)(2,1)S(1)}, bf16[256,256]{1,0:T(8,128)(2,1)S(1)}, u32[]{:S(2)}, u32[]{:S(2)}) collective-permute-start(bf16[256,256]{1,0:T(8,128)(2,1)S(1)} %get-tuple-element.18), channel_id=1, source_target_pairs={{0,1},{1,0},{2,3},{3,2},{4,5},{5,4},{6,7},{7,6},{8,9},{9,8},{10,11... | collective-permute-start | bytes 393224 | tf_op jit(solution)/shard_map/ppermute | solution.py:24
  18.5 5.7 %copy-start.1 = (bf16[256,256]{1,0:T(8,128)(2,1)S(1)}, bf16[256,256]{1,0:T(8,128)(2,1)}, u32[]{:S(2)}) copy-start(bf16[256,256]{1,0:T(8,128)(2,1)} %weight.1) | copy-start | bytes 393220
  18.5 5.7 %copy-start.3 = (bf16[128,256]{1,0:T(8,128)(2,1)S(1)}, bf16[128,256]{1,0:T(8,128)(2,1)}, u32[]{:S(2)}) copy-start(bf16[128,256]{1,0:T(8,128)(2,1)} %refs_0_.1) | copy-start | bytes 196612
  18.5 5.6 %collective-permute-start.9 = (bf16[256,256]{1,0:T(8,128)(2,1)S(1)}, bf16[256,256]{1,0:T(8,128)(2,1)S(1)}, u32[]{:S(2)}, u32[]{:S(2)}) collective-permute-start(bf16[256,256]{1,0:T(8,128)(2,1)S(1)} %shard_map.90.half), channel_id=1, source_target_pairs={{0,2},{1,3},{2,0},{3,1},{4,6},{5,7},{6,4},{7,5},{8,10},{9,11},{10,... | collective-permute-start | bytes 393224 | tf_op jit(solution)/shard_map/ppermute | solution.py:24
  24.6 1.5 %collective-permute-start.10 = (bf16[384,256]{1,0:T(8,128)(2,1)S(1)}, bf16[384,256]{1,0:T(8,128)(2,1)S(1)}, u32[]{:S(2)}, u32[]{:S(2)}) collective-permute-start(bf16[384,256]{1,0:T(8,128)(2,1)S(1)} %get-tuple-element.20.refs_1_), channel_id=1, source_target_pairs={{0,1},{1,0},{2,3},{3,2},{4,5},{5,4},{6,7},{7,6},{8,9},{9,8},{10,11... | collective-permute-start | bytes 589832 | tf_op jit(solution)/shard_map/ppermute | solution.py:24
  26.5 6.5 %collective-permute-start.14 = (bf16[256,256]{1,0:T(8,128)(2,1)S(1)}, bf16[256,256]{1,0:T(8,128)(2,1)S(1)}, u32[]{:S(2)}, u32[]{:S(2)}) collective-permute-start(bf16[256,256]{1,0:T(8,128)(2,1)S(1)} %get-tuple-element.24), channel_id=1, source_target_pairs={{0,4},{4,0},{8,12},{12,8},{16,20},{20,16},{24,28},{28,24},{1,5},{5... | collective-permute-start | bytes 393224 | tf_op jit(solution)/shard_map/ppermute | solution.py:22
  27.4 7.5 %collective-permute-start.19 = (bf16[256,256]{1,0:T(8,128)(2,1)S(1)}, bf16[256,256]{1,0:T(8,128)(2,1)S(1)}, u32[]{:S(2)}, u32[]{:S(2)}) collective-permute-start(bf16[256,256]{1,0:T(8,128)(2,1)S(1)} %get-tuple-element.28), channel_id=1, source_target_pairs={{0,4},{4,0},{8,12},{12,8},{16,20},{20,16},{24,28},{28,24},{1,5},{5... | collective-permute-start | bytes 393224 | tf_op jit(solution)/shard_map/ppermute | solution.py:22
  28.6 8.2 %collective-permute-start.11 = (bf16[128,256]{1,0:T(8,128)(2,1)S(1)}, bf16[128,256]{1,0:T(8,128)(2,1)S(1)}, u32[]{:S(2)}, u32[]{:S(2)}) collective-permute-start(bf16[128,256]{1,0:T(8,128)(2,1)S(1)} %get-tuple-element.22.refs_0_), channel_id=1, source_target_pairs={{0,8},{4,12},{8,0},{12,4},{16,24},{20,28},{24,16},{28,20},{1,9},{5... | collective-permute-start | bytes 196616 | tf_op jit(solution)/shard_map/ppermute | solution.py:22
  29.8 8.8 %collective-permute-start.12 = (bf16[128,256]{1,0:T(8,128)(2,1)S(1)}, bf16[128,256]{1,0:T(8,128)(2,1)S(1)}, u32[]{:S(2)}, u32[]{:S(2)}) collective-permute-start(bf16[128,256]{1,0:T(8,128)(2,1)S(1)} %get-tuple-element.22.refs_0_), channel_id=1, source_target_pairs={{0,16},{4,20},{8,24},{12,28},{16,0},{20,4},{24,8},{28,12},{1,17},{... | collective-permute-start | bytes 196616 | tf_op jit(solution)/shard_map/ppermute | solution.py:22
  32.2 6.3 %collective-permute-start.13 = (bf16[128,256]{1,0:T(8,128)(2,1)S(1)}, bf16[128,256]{1,0:T(8,128)(2,1)S(1)}, u32[]{:S(2)}, u32[]{:S(2)}) collective-permute-start(bf16[128,256]{1,0:T(8,128)(2,1)S(1)} %get-tuple-element.22.refs_0_), channel_id=1, source_target_pairs={{0,24},{4,28},{8,16},{12,20},{16,8},{20,12},{24,0},{28,4},{1,25},{... | collective-permute-start | bytes 196616 | tf_op jit(solution)/shard_map/ppermute | solution.py:22
  33.0 5.5 %collective-permute-start.15 = (bf16[128,256]{1,0:T(8,128)(2,1)S(1)}, bf16[128,256]{1,0:T(8,128)(2,1)S(1)}, u32[]{:S(2)}, u32[]{:S(2)}) collective-permute-start(bf16[128,256]{1,0:T(8,128)(2,1)S(1)} %get-tuple-element.25), channel_id=1, source_target_pairs={{0,8},{4,12},{8,0},{12,4},{16,24},{20,28},{24,16},{28,20},{1,9},{5... | collective-permute-start | bytes 196616 | tf_op jit(solution)/shard_map/ppermute | solution.py:22
  35.0 8.2 %collective-permute-start.20 = (bf16[128,256]{1,0:T(8,128)(2,1)S(1)}, bf16[128,256]{1,0:T(8,128)(2,1)S(1)}, u32[]{:S(2)}, u32[]{:S(2)}) collective-permute-start(bf16[128,256]{1,0:T(8,128)(2,1)S(1)} %get-tuple-element.29), channel_id=1, source_target_pairs={{0,16},{4,20},{8,24},{12,28},{16,0},{20,4},{24,8},{28,12},{1,17},{... | collective-permute-start | bytes 196616 | tf_op jit(solution)/shard_map/ppermute | solution.py:22
  36.8 6.4 %collective-permute-start.21 = (bf16[128,256]{1,0:T(8,128)(2,1)S(1)}, bf16[128,256]{1,0:T(8,128)(2,1)S(1)}, u32[]{:S(2)}, u32[]{:S(2)}) collective-permute-start(bf16[128,256]{1,0:T(8,128)(2,1)S(1)} %get-tuple-element.30), channel_id=1, source_target_pairs={{0,24},{4,28},{8,16},{12,20},{16,8},{20,12},{24,0},{28,4},{1,25},{... | collective-permute-start | bytes 196616 | tf_op jit(solution)/shard_map/ppermute | solution.py:22
  38.6 4.6 %collective-permute-start.16 = (bf16[128,256]{1,0:T(8,128)(2,1)S(1)}, bf16[128,256]{1,0:T(8,128)(2,1)S(1)}, u32[]{:S(2)}, u32[]{:S(2)}) collective-permute-start(bf16[128,256]{1,0:T(8,128)(2,1)S(1)} %shard_map.95.refs_0_), channel_id=1, source_target_pairs={{0,4},{4,0},{8,12},{12,8},{16,20},{20,16},{24,28},{28,24},{1,5},{5... | collective-permute-start | bytes 196616 | tf_op jit(solution)/shard_map/ppermute | solution.py:22
  39.8 3.4 %collective-permute-start.17 = (bf16[128,256]{1,0:T(8,128)(2,1)S(1)}, bf16[128,256]{1,0:T(8,128)(2,1)S(1)}, u32[]{:S(2)}, u32[]{:S(2)}) collective-permute-start(bf16[128,256]{1,0:T(8,128)(2,1)S(1)} %shard_map.95.refs_0_), channel_id=1, source_target_pairs={{0,1},{1,0},{2,3},{3,2},{4,5},{5,4},{6,7},{7,6},{8,9},{9,8},{10,11... | collective-permute-start | bytes 196616 | tf_op jit(solution)/shard_map/ppermute | solution.py:24
  39.8 4.0 %collective-permute-start.18 = (bf16[128,256]{1,0:T(8,128)(2,1)S(1)}, bf16[128,256]{1,0:T(8,128)(2,1)S(1)}, u32[]{:S(2)}, u32[]{:S(2)}) collective-permute-start(bf16[128,256]{1,0:T(8,128)(2,1)S(1)} %shard_map.95.refs_0_), channel_id=1, source_target_pairs={{0,5},{1,4},{2,7},{3,6},{4,1},{5,0},{6,3},{7,2},{8,13},{9,12},{10,... | collective-permute-start | bytes 196616 | tf_op jit(solution)/shard_map/ppermute | solution.py:28
